TPU v7x, 32 devices: a whole 2x2x4 slice. The times are simulated.
32 devices in a mesh: branch: 8 (over y, x, core), head: 4 (over z).
Axes of the slice: x: 2, y: 2, z: 4, core: 2. Of those that a mesh axis runs over, the one named last changes fastest.
Arguments:
- queries: bfloat16 [4, 8, 256, 8192], P(None, 'branch', None, 'head'), may hold values from -96 to 96
- key_rows: bfloat16 [4, 8, 256, 1024], P(None, 'branch', None, 'head'), may hold values from -4 to 4
- value_rows: bfloat16 [4, 8, 256, 1024], P(None, 'branch', None, 'head'), may hold values from -5 to 5
- cotangent: bfloat16 [4, 8, 256, 8192], P(None, 'branch', None, 'head'), may hold values from -6 to 6
- out_weight: bfloat16 [8192, 8192], P('head'), may hold values from -0.0625 to 0.0625
- parents: int32 [3, 8], replicated, may hold values from 0 to 7
- seg_len: int32 [4, 8], replicated, may hold values from 128 to 256, as said below
Outputs:
- query_grad: bfloat16 [4, 8, 256, 8192], P(None, 'branch', None, 'head')
- key_grad: bfloat16 [4, 8, 256, 1024], P(None, 'branch', None, 'head')
- value_grad: bfloat16 [4, 8, 256, 1024], P(None, 'branch', None, 'head')
Inputs may be any that keep to these rules, and one draw needn't show every extreme that they name: parents[m, j] is the node of level m that node j of level m + 1 continues; a node may have many children or none. `seg_len`: some node uses all 256 slots in every draw.
All inputs are finite; a program needn't handle non-finite values.
Results may differ from a plain program's by a relative error of at most 0.015.
Values may be sent and summed in bfloat16 or wider, within the bound.
A program may use at most 192 MiB of HBM per device.

v0:
```python
import jax
import jax.numpy as jnp
from jax import lax
from jax.sharding import PartitionSpec as P

HD = 128


masked_score = -1e30


def pick_row(table, index_value):
    return lax.dynamic_index_in_dim(table, index_value, 0, keepdims=False)


def local(queries, key_rows, value_rows, cotangent, out_weight, parents, seg_len):
    levels, _, seg_rows, q_width = queries.shape
    kv_width = key_rows.shape[3]
    kv_local = kv_width // HD
    group_size = q_width // kv_width
    node_count = parents.shape[1]
    row_count = levels * seg_rows
    logit_scale = 1.0 / HD**0.5
    my_node = lax.axis_index("branch")
    piece = lax.all_gather(cotangent, "head", axis=3, tiled=True)
    piece_width = piece.shape[3]
    product = lax.dot_general(
        piece.reshape(row_count, piece_width),
        out_weight,
        (((1,), (1,)), ((), ())),
        preferred_element_type=jnp.float32,
    )
    dout_all = product
    dout_all = dout_all.astype(jnp.bfloat16).reshape(levels, seg_rows, q_width)
    key_all, value_all = (
        lax.all_gather(key_rows, "branch", axis=1, tiled=True),
        lax.all_gather(value_rows, "branch", axis=1, tiled=True),
    )
    positions = jnp.arange(seg_rows)
    grad_terms = jnp.zeros((levels, node_count, seg_rows, 2 * kv_width), jnp.float32)
    query_levels = [None] * levels
    for level_index in reversed(range(levels)):
        lineage = [None] * (level_index + 1)
        lineage[level_index] = my_node
        for ancestor_level in reversed(range(level_index)):
            lineage[ancestor_level] = pick_row(parents[ancestor_level], lineage[ancestor_level + 1])
        key_blocks = []
        value_blocks = []
        allowed_blocks = []
        for ancestor_level in range(level_index):
            key_blocks.append(pick_row(key_all[ancestor_level], lineage[ancestor_level]))
            value_blocks.append(pick_row(value_all[ancestor_level], lineage[ancestor_level]))
            length = pick_row(seg_len[ancestor_level], lineage[ancestor_level])
            allowed_blocks.append(
                jnp.broadcast_to(positions[None, :] < length, (seg_rows, seg_rows))
            )
        own_length = pick_row(seg_len[level_index], my_node)
        key_blocks.append(key_rows[level_index, 0])
        value_blocks.append(value_rows[level_index, 0])
        allowed_blocks.append(
            (positions[None, :] <= positions[:, None]) & (positions[None, :] < own_length)
        )
        key_cat = jnp.concatenate(key_blocks, axis=0)
        value_cat = jnp.concatenate(value_blocks, axis=0)
        allowed = jnp.concatenate(allowed_blocks, axis=1)
        key_count = key_cat.shape[0]
        key_heads = key_cat.reshape(key_count, kv_local, HD)
        value_heads = value_cat.reshape(key_count, kv_local, HD)
        query_heads = queries[level_index, 0].reshape(seg_rows, kv_local, group_size, HD)
        query_valid = positions < own_length
        dout_rows = jnp.where(
            query_valid[:, None], dout_all[level_index], jnp.zeros_like(dout_all[level_index])
        )
        dout_heads = dout_rows.reshape(seg_rows, kv_local, group_size, HD)
        score_matrix = (
            jnp.einsum("qngd,knd->ngqk", query_heads, key_heads, preferred_element_type=jnp.float32)
            * logit_scale
        )
        score_matrix = jnp.where(allowed[None, None], score_matrix, masked_score)
        maximum = jnp.max(score_matrix, axis=-1, keepdims=True)
        exponent = jnp.exp(score_matrix - maximum)
        softmax = exponent / jnp.sum(exponent, axis=-1, keepdims=True)
        probability_narrow = softmax.astype(jnp.bfloat16)
        attention_weights = jnp.einsum(
            "ngqk,knd->qngd", probability_narrow, value_heads, preferred_element_type=jnp.float32
        )
        delta_rows = jnp.sum(dout_heads.astype(jnp.float32) * attention_weights, axis=-1)
        probability_gradient = jnp.einsum(
            "qngd,knd->ngqk", dout_heads, value_heads, preferred_element_type=jnp.float32
        )
        dscores = softmax * (probability_gradient - jnp.transpose(delta_rows, (1, 2, 0))[..., None])
        score_gradient_narrow = dscores.astype(jnp.bfloat16)
        query_portion = (
            jnp.einsum(
                "ngqk,knd->qngd",
                score_gradient_narrow,
                key_heads,
                preferred_element_type=jnp.float32,
            )
            * logit_scale
        )
        query_levels[level_index] = query_portion.astype(jnp.bfloat16).reshape(1, seg_rows, q_width)
        key_portion = (
            jnp.einsum(
                "ngqk,qngd->knd",
                score_gradient_narrow,
                query_heads,
                preferred_element_type=jnp.float32,
            )
            * logit_scale
        )
        value_portion = jnp.einsum(
            "ngqk,qngd->knd", probability_narrow, dout_heads, preferred_element_type=jnp.float32
        )
        key_value_grad = jnp.concatenate(
            [key_portion.reshape(key_count, kv_width), value_portion.reshape(key_count, kv_width)],
            axis=1,
        )
        for ancestor_level in range(level_index + 1):
            block = key_value_grad[ancestor_level * seg_rows : (ancestor_level + 1) * seg_rows]
            corner = (
                jnp.int32(ancestor_level),
                lineage[ancestor_level],
                jnp.int32(0),
                jnp.int32(0),
            )
            current = lax.dynamic_slice(grad_terms, corner, (1, 1, seg_rows, 2 * kv_width))
            grad_terms = lax.dynamic_update_slice(grad_terms, current + block[None, None], corner)
    summed = lax.psum_scatter(grad_terms, "branch", scatter_dimension=1, tiled=True)
    query_grad = jnp.stack(query_levels, axis=0)
    key_grad = summed[..., :kv_width].astype(jnp.bfloat16)
    value_grad = summed[..., kv_width:].astype(jnp.bfloat16)
    return (query_grad, key_grad, value_grad)


def solution(mesh):
    in_specs = (
        P(None, "branch", None, "head"),
        P(None, "branch", None, "head"),
        P(None, "branch", None, "head"),
        P(None, "branch", None, "head"),
        P("head", None),
        P(),
        P(),
    )
    out_specs = (
        P(None, "branch", None, "head"),
        P(None, "branch", None, "head"),
        P(None, "branch", None, "head"),
    )
    return jax.shard_map(local, mesh=mesh, in_specs=in_specs, out_specs=out_specs, check_vma=False)
```

profile of v0, /device:TPU:0, one launch (start us, length us, event | category | flops | bytes accessed | tf_op | source)
XLA Modules:
  0.0 889.2 jit_solution(11068471262190638171)
XLA Ops:
  7.2 2.0 copy.140
  9.3 2.1 copy.145
  28.8 3.9 fusion.133
  51.9 4.4 fusion.144
  56.4 4.1 fusion.37
  60.4 3.6 fusion.135
  64.1 25.1 %all-gather.8.cloned.1.call-done = bf16[4,8,256,256]{2,3,1,0:T(8,128)(2,1)} async-done(((bf16[4,1,256,256]{2,3,1,0:T(8,128)(2,1)}), bf16[4,8,256,256]{2,3,1,0:T(8,128)(2,1)}) %all-gather.8.cloned.1.call-update) | async-done | bytes 4194320 | tf_op jit(solution)/shard_map/all_gather | solution.py:37
  89.2 3.5 fusion.134
  100.3 2.3 constant_dynamic-slice_fusion.22
  116.0 7.7 fusion.143
  123.8 10.6 %fusion.142 = (f32[2,8,256]{2,1,0:T(8,128)}, f32[2,8,256,768]{2,3,1,0:T(8,128)}) fusion(pred[256,768]{0,1:T(8,128)(4,1)} %pad_add_fusion.1, bf16[256,2,8,128]{0,3,2,1:T(8,128)(2,1)} %bitcast.412, bf16[256,2,128]{2,0,1:T(8,128)(2,1)S(1)} %copy.170, bf16[256,2,128]{2,0,1:T(8,128)(2,1)} %copy.169, bf16[256,2,128]{2,0,1:T(8,128)(2,1)} %copy.168), kind=kOutput, calls=%fused_computation.235 | convolution fusion | flops 819069696 | bytes 14237696 | tf_op jit(solution)/shard_map/sub | solution.py:81
  134.3 21.4 %fusion.141 = (f32[2,8,256]{2,1,0:T(8,128)S(1)}, f32[2,8,256,1024]{2,3,1,0:T(8,128)}) fusion(pred[256,1024]{0,1:T(8,128)(4,1)} %pad_add_fusion, bf16[256,2,8,128]{0,3,2,1:T(8,128)(2,1)S(1)} %bitcast.396, bf16[256,2,128]{2,0,1:T(8,128)(2,1)S(1)} %copy.187, bf16[256,2,128]{2,0,1:T(8,128)(2,1)S(1)} %copy.186, bf16[256,2,128]{2,0,1:T(8,128)(2,1)} %copy.185, ...), kind=kOutput, calls=%fused_computation.234 | convolution fusion | flops 1092617216 | bytes 18628608 | tf_op jit(solution)/shard_map/sub | solution.py:81
  155.8 6.3 fusion.26
  162.1 8.6 fusion.20
  170.7 9.2 %fusion.15 = bf16[2,8,256,1024]{2,3,1,0:T(8,128)(2,1)} fusion(f32[2,8,256,1024]{2,3,1,0:T(8,128)} %get-tuple-element.59, f32[2,8,256]{2,1,0:T(8,128)S(1)} %get-tuple-element.58), kind=kLoop, calls=%fused_computation.25 | loop fusion | flops 8388608 | bytes 25182208 | tf_op jit(solution)/shard_map/convert_element_type | solution.py:83
  180.0 197.6 %all-gather.4.cloned.1.call-done = bf16[4,1,256,8192]{3,2,1,0:T(8,128)(2,1)} async-done(((bf16[4,1,256,2048]{3,2,1,0:T(8,128)(2,1)}), bf16[4,1,256,8192]{3,2,1,0:T(8,128)(2,1)}) %all-gather.4.cloned.1.call-update) | async-done | bytes 16777232 | tf_op jit(solution)/shard_map/all_gather | solution.py:25
  377.6 44.5 %convolution_convert_fusion = bf16[1024,2048]{1,0:T(8,128)(2,1)} fusion(bf16[1024,8192]{1,0:T(8,128)(2,1)} %bitcast.450, bf16[2048,8192]{1,0:T(8,128)(2,1)} %param.11), kind=kOutput, calls=%fused_computation.42 | convolution fusion | flops 34361835520 | bytes 54525952 | tf_op jit(solution)/shard_map/dot_general | solution.py:27
  422.1 4.0 fusion.132
  427.4 3.6 fusion.46
  430.9 2.4 fusion.31
  438.6 4.4 fusion.47
  443.0 3.0 fusion.30
  446.0 4.2 fusion.11
  450.2 2.3 fusion.42
  455.9 6.0 fusion.48
  463.1 5.7 fusion.8
  468.8 3.0 fusion.41
  471.8 2.0 multiply_convert_fusion.1
  474.4 7.5 fusion.49
  482.0 4.7 fusion.28
  486.8 8.2 fusion.5
  495.0 3.8 fusion.40
  498.8 2.3 multiply_convert_fusion
  506.5 2.3 copy.202
  508.8 2.0 copy.215
  513.6 2.3 copy.211
  520.5 7.9 broadcast_in_dim.190
  529.3 1.9 fusion.72
  531.2 1.9 fusion.65
  533.2 2.0 fusion.81
  535.1 1.9 fusion.61
  537.1 1.9 fusion.57
  539.0 1.9 fusion.78
  540.9 1.9 fusion.53
  544.7 1.9 fusion.83
  546.6 329.6 %all-reduce.2 = bf16[4,8,256,512]{3,2,1,0:T(8,128)(2,1)} all-reduce(f32[4,8,256,512]{3,2,1,0:T(8,128)} %fusion.83), channel_id=2, replica_groups=mesh['branch'=8,'head'=4] {'branch'}, use_global_device_ids=true, to_apply=%region_12.13.clone | all-reduce | flops 4194304 | bytes 25165824
  876.2 1.9 dynamic-slice_convert_fusion
  879.2 3.3 pad_maximum_fusion
  (205 shorter events, 74.0 us)
Async XLA Ops:
  7.2 5.0 copy-start.55
  7.2 53.3 %all-gather.6.cloned.1.call-start = ((), (), s32[]{:S(2)}) async-start(), calls=%async_computation.1 | async-start | bytes 4718592 | tf_op jit(solution)/shard_map/all_gather | solution.py:36
  9.3 18.5 %copy-start.2 = (bf16[4,1,256,256]{2,3,1,0:T(8,128)(2,1)S(1)}, bf16[4,1,256,256]{2,3,1,0:T(8,128)(2,1)}, u32[]{:S(2)}) copy-start(bf16[4,1,256,256]{2,3,1,0:T(8,128)(2,1)} %copy.140) | copy-start | bytes 1572868
  9.3 79.9 %all-gather.8.cloned.1.call-start = ((), (), s32[]{:S(2)}) async-start(), calls=%async_computation.2 | async-start | bytes 4718592 | tf_op jit(solution)/shard_map/all_gather | solution.py:37
  11.4 366.1 %all-gather.4.cloned.1.call-start = ((), (), s32[]{:S(2)}) async-start(), calls=%async_computation | async-start | bytes 20971520 | tf_op jit(solution)/shard_map/all_gather | solution.py:25
  27.8 24.2 %copy-start.30 = (bf16[1,1,256,256]{2,3,1,0:T(8,128)(2,1)}, bf16[1,1,256,256]{2,3,1,0:T(8,128)(2,1)S(1)}, u32[]{:S(2)}) copy-start(bf16[1,1,256,256]{2,3,1,0:T(8,128)(2,1)S(1)} %get-tuple-element.33) | copy-start | bytes 393220
  27.9 106.4 %copy-start.18 = (bf16[256,2,128]{2,0,1:T(8,128)(2,1)}, bf16[256,2,128]{2,0,1:T(8,128)(2,1)S(1)}, u32[]{:S(2)}) copy-start(bf16[256,2,128]{2,0,1:T(8,128)(2,1)S(1)} %copy.187) | copy-start | bytes 393220
  28.0 95.7 %copy-start.20 = (bf16[256,2,128]{2,0,1:T(8,128)(2,1)}, bf16[256,2,128]{2,0,1:T(8,128)(2,1)S(1)}, u32[]{:S(2)}) copy-start(bf16[256,2,128]{2,0,1:T(8,128)(2,1)S(1)} %copy.170) | copy-start | bytes 393220
  32.7 7.5 copy-start.54
  37.6 96.8 %copy-start.3 = (bf16[1,1,256,2048]{2,3,1,0:T(8,128)(2,1)}, bf16[1,1,256,2048]{2,3,1,0:T(8,128)(2,1)S(1)}, u32[]{:S(2)}) copy-start(bf16[1,1,256,2048]{2,3,1,0:T(8,128)(2,1)S(1)} %copy.295) | copy-start | bytes 3145732
  43.0 6.3 copy-start.48
  43.6 5.8 copy-start.52
  100.3 34.0 %copy-start.22 = (bf16[256,2,128]{2,0,1:T(8,128)(2,1)}, bf16[256,2,128]{2,0,1:T(8,128)(2,1)S(1)}, u32[]{:S(2)}) copy-start(bf16[256,2,128]{2,0,1:T(8,128)(2,1)S(1)} %copy.186) | copy-start | bytes 393220
  134.3 21.5 %copy-start.42 = (f32[2,8,256]{2,1,0:T(8,128)S(1)}, f32[2,8,256]{2,1,0:T(8,128)}, u32[]{:S(2)}) copy-start(f32[2,8,256]{2,1,0:T(8,128)} %get-tuple-element.62) | copy-start | bytes 49156
  155.8 14.9 %copy-start.44 = (f32[2,8,256]{2,1,0:T(8,128)}, f32[2,8,256]{2,1,0:T(8,128)S(1)}, u32[]{:S(2)}) copy-start(f32[2,8,256]{2,1,0:T(8,128)S(1)} %get-tuple-element.58) | copy-start | bytes 49156
  155.8 6.3 copy-start.46
  422.1 5.3 copy-start.57
  422.1 8.8 copy-start.41
  427.4 5.9 copy-start.7
  427.4 5.9 copy-start.15
  435.2 7.8 copy-start.34
  435.2 7.8 copy-start.40
  438.5 7.4 copy-start.43
  446.0 6.5 copy-start.28
  446.0 6.5 copy-start.29
  450.2 5.7 copy-start.49
  452.5 9.4 %slice-start = ((s8[6291456]{0:T(1024)(128)(4,1)}), s8[2097152]{0:T(1024)(128)(4,1)S(1)}, s32[]{:S(2)}) async-start(s8[6291456]{0:T(1024)(128)(4,1)} %bitcast.394), calls=%async_computation.3 | async-start | bytes 4194304
  454.4 7.5 copy-start.33
  455.9 6.0 copy-start.37
  455.9 6.0 copy-start.39
  455.9 6.0 slice-start.1
  463.0 5.7 copy-start.8
  468.8 5.1 copy-start.11
  473.9 8.1 copy-start.32
  473.9 8.1 copy-start.35
  473.9 8.1 copy-start.36
  473.9 8.1 copy-start.38
  474.4 12.3 %copy-start.14 = (bf16[256,2048]{0,1:T(8,128)(2,1)}, bf16[256,2048]{0,1:T(8,128)(2,1)S(1)}, u32[]{:S(2)}) copy-start(bf16[256,2048]{0,1:T(8,128)(2,1)S(1)} %copy.287) | copy-start | bytes 3145732
  486.8 8.2 copy-start.4
  501.1 11.1 %copy-start.13 = (bf16[2,128,8,256]{3,1,2,0:T(8,128)(2,1)S(1)}, bf16[2,128,8,256]{3,1,2,0:T(8,128)(2,1)}, u32[]{:S(2)}) copy-start(bf16[2,128,8,256]{3,1,2,0:T(8,128)(2,1)} %multiply_convert_fusion.1) | copy-start | bytes 3145732
  504.4 13.1 %copy-start.6 = (bf16[2,128,8,256]{3,1,2,0:T(8,128)(2,1)S(1)}, bf16[2,128,8,256]{3,1,2,0:T(8,128)(2,1)}, u32[]{:S(2)}) copy-start(bf16[2,128,8,256]{3,1,2,0:T(8,128)(2,1)} %multiply_convert_fusion) | copy-start | bytes 3145732
  528.5 6.7 copy-start
  533.2 7.8 copy-start.1
  535.1 9.6 %copy-start.16 = (f32[256,256]{1,0:T(8,128)S(1)}, f32[256,256]{1,0:T(8,128)}, u32[]{:S(2)}) copy-start(f32[256,256]{1,0:T(8,128)} %copy.220) | copy-start | bytes 786436
  535.1 9.6 %copy-start.17 = (f32[256,256]{1,0:T(8,128)S(1)}, f32[256,256]{1,0:T(8,128)}, u32[]{:S(2)}) copy-start(f32[256,256]{1,0:T(8,128)} %copy.219) | copy-start | bytes 786436
  546.6 332.6 %copy-start.9 = (bf16[1,1,256,2048]{3,2,1,0:T(8,128)(2,1)S(1)}, bf16[1,1,256,2048]{3,2,1,0:T(8,128)(2,1)}, u32[]{:S(2)}) copy-start(bf16[1,1,256,2048]{3,2,1,0:T(8,128)(2,1)} %copy.201) | copy-start | bytes 3145732
  546.6 332.6 %copy-start.10 = (bf16[1,1,256,2048]{3,2,1,0:T(8,128)(2,1)S(1)}, bf16[1,1,256,2048]{3,2,1,0:T(8,128)(2,1)}, u32[]{:S(2)}) copy-start(bf16[1,1,256,2048]{3,2,1,0:T(8,128)(2,1)} %copy.202) | copy-start | bytes 3145732
  546.6 332.6 %copy-start.12 = (bf16[1,1,256,2048]{3,2,1,0:T(8,128)(2,1)S(1)}, bf16[1,1,256,2048]{3,2,1,0:T(8,128)(2,1)}, u32[]{:S(2)}) copy-start(bf16[1,1,256,2048]{3,2,1,0:T(8,128)(2,1)} %copy.203) | copy-start | bytes 3145732
  (16 other events, 54.9 us)
Sparse Core Ops, SparseCore 0:
  10.5 39.4 all-gather.5
  52.4 36.7 all-gather.7
  90.8 286.7 all-gather.3
where the time goes:
time: 901 us; the launch traced here: 889 us
  blocking collectives  330 us (37%)
  waiting for transfers between devices  223 us (25%)
  matrix products  158 us (18%)
  local copies, waits for them, and re-layouts  92 us (10%)
  other arithmetic  59.8 us (7%)
  between operations  26.3 us (3%)
    unnamed x1, blocking collectives  330 us
    all_gather x1, waiting for transfers between devices, local(): piece = lax.all_gather(cotangent, 'head', axis=3, tiled=True)  198 us
    dot_general x1, matrix products, local(): lax.dot_general(piece.reshape(row_count, piece_width), out_weight, (((1,)...  44.5 us
    sub x4, matrix products, local(): exponent = jnp.exp(score_matrix - maximum)  44.2 us
    convert_element_type x4, other arithmetic, local(): probability_narrow = softmax.astype(jnp.bfloat16)  28.2 us
    all_gather x1, waiting for transfers between devices, local(): lax.all_gather(value_rows, 'branch', axis=1, tiled=True)  25.1 us
    dot_general x4, matrix products, local(): jnp.einsum('ngqk,qngd->knd', probability_narrow, dout_heads, preferred_el...  21.5 us
    dot_general x4, matrix products, local(): jnp.einsum('qngd,knd->ngqk', dout_heads, value_heads, preferred_element_t...  19.1 us
  transfers between devices with their start and end apart: 3, of which 2 were waited for; matrix products, arithmetic and copies ran while one was open for 15% of the time, Pallas kernels for 0%

commit v1 on v0

v1 whole, which is shorter than its diff:
```python
import functools

import jax
import jax.numpy as jnp
from jax import lax
from jax.experimental import pallas as pl
from jax.experimental.pallas import tpu as pltpu
from jax.sharding import PartitionSpec as P

HD = 128
MASKED = -1e30
NT = (((1,), (1,)), ((), ()))
NN = (((1,), (0,)), ((), ()))
TN = (((0,), (0,)), ((), ()))


def pick_row(table, index_value):
    return lax.dynamic_index_in_dim(table, index_value, 0, keepdims=False)


def attention_kernel(level, has_base, info_ref, q_ref, dout_ref, *refs):
    blocks = level + 1
    key_refs, value_refs = refs[:blocks], refs[blocks : 2 * blocks]
    dq_ref, dk_ref, dv_ref = refs[2 * blocks + has_base :]
    seg = dout_ref.shape[0]
    scale = 1.0 / HD**0.5
    q = q_ref[...].reshape(seg, HD)
    own_len = info_ref[4 + level]
    dout = dout_ref[...]
    row = lax.broadcasted_iota(jnp.int32, (seg, HD), 0)
    dout = jnp.where(row < own_len, dout, jnp.zeros_like(dout))
    keys = [ref[...].reshape(seg, HD) for ref in key_refs]
    values = [ref[...].reshape(seg, HD) for ref in value_refs]
    key_pos = lax.broadcasted_iota(jnp.int32, (seg, seg), 0)
    query_pos = lax.broadcasted_iota(jnp.int32, (seg, seg), 1)

    def dot(a, b, dims):
        return lax.dot_general(a, b, dims, preferred_element_type=jnp.float32)

    scores = []
    for m in range(blocks):
        allowed = key_pos < info_ref[4 + m]
        if m == level:
            allowed = allowed & (key_pos <= query_pos)
        scores.append(jnp.where(allowed, dot(keys[m], q, NT) * scale, MASKED))
    top = functools.reduce(jnp.maximum, [jnp.max(s, axis=0, keepdims=True) for s in scores])
    exps = [jnp.exp(s - top) for s in scores]
    total = functools.reduce(jnp.add, [jnp.sum(e, axis=0, keepdims=True) for e in exps])
    inverse = 1.0 / total
    probs = [e * inverse for e in exps]
    narrow = [p.astype(jnp.bfloat16) for p in probs]
    dprobs = [dot(v, dout, NT) for v in values]
    delta = functools.reduce(
        jnp.add,
        [
            jnp.sum(pb.astype(jnp.float32) * dp, axis=0, keepdims=True)
            for pb, dp in zip(narrow, dprobs)
        ],
    )

    @pl.when(pl.program_id(1) == 0)
    def _():
        dk_ref[...] = jnp.zeros_like(dk_ref)
        dv_ref[...] = jnp.zeros_like(dv_ref)

    dq = jnp.zeros((HD, seg), jnp.float32)
    for m in range(blocks):
        ds = (probs[m] * (dprobs[m] - delta)).astype(jnp.bfloat16)
        dk_ref[m] += dot(ds, q, NN) * scale
        dv_ref[m] += dot(narrow[m], dout, NN)
        dq = dq + dot(keys[m], ds, TN)
    dq_ref[...] = (dq * scale).T.astype(jnp.bfloat16).reshape(dq_ref.shape)


def attention_level(level, info, queries, dout, key_rows, value_rows, kv_all, base):
    levels, _, seg, q_width = queries.shape
    kv_width = key_rows.shape[3]
    kv_local = kv_width // HD
    group = q_width // kv_width
    blocks = level + 1

    def gathered(kind, m):
        return pl.BlockSpec(
            (1, 1, 1, seg, HD), lambda n, g, info, m=m, k=kind: (info[m], m, k, 0, n)
        )

    q_spec = pl.BlockSpec((1, 1, seg, HD), lambda n, g, info: (level, 0, 0, n * group + g))
    own_spec = pl.BlockSpec((1, 1, seg, HD), lambda n, g, info: (level, 0, 0, n))
    head_spec = pl.BlockSpec((seg, HD), lambda n, g, info: (0, n * group + g))
    grad_spec = pl.BlockSpec((blocks, seg, HD), lambda n, g, info: (0, 0, n))
    in_specs = [q_spec, head_spec]
    in_specs += [gathered(0, m) for m in range(level)] + [own_spec]
    in_specs += [gathered(1, m) for m in range(level)] + [own_spec]
    operands = [queries, dout] + [kv_all] * level + [key_rows] + [kv_all] * level + [value_rows]
    aliases = {}
    if base is not None:
        in_specs.append(pl.BlockSpec(memory_space=pl.ANY))
        operands.append(base)
        aliases = {len(operands): 0}
    grad_shape = jax.ShapeDtypeStruct((blocks, seg, kv_width), jnp.float32)
    products = 5 * 2 * seg * seg * HD * blocks * kv_local * group
    return pl.pallas_call(
        functools.partial(attention_kernel, level, int(base is not None)),
        grid_spec=pltpu.PrefetchScalarGridSpec(
            num_scalar_prefetch=1,
            grid=(kv_local, group),
            in_specs=in_specs,
            out_specs=[q_spec, grad_spec, grad_spec],
        ),
        out_shape=[jax.ShapeDtypeStruct(queries.shape, jnp.bfloat16), grad_shape, grad_shape],
        input_output_aliases=aliases,
        compiler_params=pltpu.CompilerParams(vmem_limit_bytes=40 * 1024 * 1024),
        cost_estimate=pl.CostEstimate(
            flops=4 * products,
            bytes_accessed=3 * seg * q_width * 2,
            transcendentals=seg * seg * blocks * kv_local * group,
        ),
        name="attention_level",
    )(info, *operands)


def local(node_count, queries, key_rows, value_rows, cotangent, out_weight, parents, seg_len):
    levels, _, seg, q_width = queries.shape
    bits = node_count.bit_length() - 1
    me = lax.axis_index("branch")

    def swap(array, bit):
        pairs = [(i, i ^ (1 << bit)) for i in range(node_count)]
        return lax.ppermute(array, "branch", pairs)

    gathered = [None] * levels
    for level in reversed(range(levels)):
        gathered[level] = lax.all_gather(cotangent[level, 0], "head", axis=1, tiled=True)

    kv_all = jnp.stack([key_rows[: levels - 1, 0], value_rows[: levels - 1, 0]], axis=1)[None]
    for bit in reversed(range(bits)):
        kv_all = jnp.concatenate([kv_all, swap(kv_all, bit)], axis=0)

    offsets = []
    infos = []
    for level in range(levels):
        lineage = [None] * (level + 1)
        lineage[level] = me
        for m in reversed(range(level)):
            lineage[m] = pick_row(parents[m], lineage[m + 1])
        relative = [node ^ me for node in lineage]
        slots = [
            sum(((r >> b) & 1) << (bits - 1 - b) for b in range(bits)) for r in relative
        ]
        lengths = [pick_row(seg_len[m], lineage[m]) for m in range(level + 1)]
        pad = [jnp.int32(0)] * (levels - 1 - level)
        infos.append(jnp.stack(slots + pad + lengths + pad).astype(jnp.int32))
        offsets.append(relative)

    key_terms = [[] for _ in range(levels)]
    key_grads = [None] * levels
    value_grads = [None] * levels
    query_grad = None
    for level in reversed(range(levels)):
        dout = lax.dot_general(
            gathered[level], out_weight, NT, preferred_element_type=jnp.float32
        ).astype(jnp.bfloat16)
        query_grad, dk, dv = attention_level(
            level, infos[level], queries, dout, key_rows, value_rows, kv_all, query_grad
        )
        own = jnp.stack([dk[level], dv[level]])
        if level < levels - 1:
            own = own + received
        key_grads[level] = own[0].astype(jnp.bfloat16)
        value_grads[level] = own[1].astype(jnp.bfloat16)
        for m in range(level):
            key_terms[m].append((offsets[level][m], dk[m], dv[m]))
        if level > 0:
            m = level - 1

            def spread(ids):
                total = jnp.zeros((len(ids), 2, seg, key_rows.shape[3]), jnp.float32)
                for offset, dk_term, dv_term in key_terms[m]:
                    hit = (jnp.array(ids, jnp.int32) == offset)[:, None, None, None]
                    total = total + jnp.where(hit, jnp.stack([dk_term, dv_term])[None], 0.0)
                return total

            keep = spread(range(0, node_count, 2))
            send = spread(range(1, node_count, 2)).astype(jnp.bfloat16)
            for bit in range(bits):
                held = keep + swap(send, bit).astype(jnp.float32)
                if bit + 1 < bits:
                    keep = held[0::2]
                    send = held[1::2].astype(jnp.bfloat16)
            received = held[0]
    key_grad = jnp.stack(key_grads)[:, None]
    value_grad = jnp.stack(value_grads)[:, None]
    return query_grad, key_grad, value_grad


def solution(mesh):
    wide = P(None, "branch", None, "head")
    in_specs = (wide, wide, wide, wide, P("head", None), P(), P())
    return jax.shard_map(
        functools.partial(local, mesh.shape["branch"]),
        mesh=mesh,
        in_specs=in_specs,
        out_specs=(wide, wide, wide),
        check_vma=False,
    )
```

time: 901 us -> 423 us (0.47); the launches traced: 889 us -> 422 us
  blocking collectives: 330 us -> 0 us
  matrix products: 158 us -> 64.4 us
  Pallas kernels: 0 us -> 74.7 us
  local copies, waits for them, and re-layouts: 92 us -> 34.3 us
  waiting for transfers between devices: 223 us -> 183 us
  other arithmetic: 59.8 us -> 22.1 us
  starting transfers between devices: 0.12 us -> 13.8 us
    unnamed x1 -> x0, blocking collectives: 330 us -> none
    all_gather x3 -> x4, waiting for transfers between devices: 223 us -> 99.5 us  [local(): lax.all_gather(cotangent[level, 0], 'head', axis=1, tiled=True)]
    ppermute x0 -> x12, waiting for transfers between devices: none -> 82.4 us  [swap(): return lax.ppermute(array, 'branch', pairs)]
    pallas_call x0 -> x4, Pallas kernels: none -> 74.7 us  [attention_level(): pl.pallas_call(functools.partial(attention_kernel, level, int(base is not...]
    dot_general x21 -> x4, matrix products: 114 us -> 64.4 us  [local(): lax.dot_general(gathered[level], out_weight, NT, preferred_element_type=j...]
    sub x4 -> x0, matrix products: 44.2 us -> none  [local(): exponent = jnp.exp(score_matrix - maximum)]
    convert_element_type x4 -> x3, other arithmetic: 28.2 us -> 4.07 us  [local(): send = spread(range(1, node_count, 2)).astype(jnp.bfloat16)]
    concatenate x19 -> x0, local copies, waits for them, and re-layouts: 20.8 us -> none  [the longest x9 10.4 us: local(): value_cat = jnp.concatenate(value_blocks, axis=0)]
  transfers between devices with their start and end apart: 3 -> 16, of which waited for: 2 -> 9; matrix products, arithmetic and copies ran while one was open for 15% -> 24% of each run, Pallas kernels for 0% -> 18%
where the time goes in v1:
time: 423 us; the launch traced here: 422 us
  waiting for transfers between devices  183 us (43%)
  Pallas kernels  74.7 us (18%)
  matrix products  64.4 us (15%)
  local copies, waits for them, and re-layouts  34.3 us (8%)
  between operations  29.6 us (7%)
  other arithmetic  22.1 us (5%)
  starting transfers between devices  13.8 us (3%)
    all_gather x4, waiting for transfers between devices, local(): lax.all_gather(cotangent[level, 0], 'head', axis=1, tiled=True)  99.5 us
    ppermute x12, waiting for transfers between devices, swap(): return lax.ppermute(array, 'branch', pairs)  82.4 us
    pallas_call x4, Pallas kernels, attention_level(): pl.pallas_call(functools.partial(attention_kernel, level, int(base is not...  74.7 us
    dot_general x4, matrix products, local(): lax.dot_general(gathered[level], out_weight, NT, preferred_element_type=j...  64.4 us
    unnamed x76, local copies, waits for them, and re-layouts  14.6 us
    ppermute x12, starting transfers between devices, swap(): return lax.ppermute(array, 'branch', pairs)  13.6 us
  transfers between devices with their start and end apart: 16, of which 9 were waited for; matrix products, arithmetic and copies ran while one was open for 24% of the time, Pallas kernels for 18%

profile of v1, /device:TPU:0, one launch (start us, length us, event | category | flops | bytes accessed | tf_op | source)
XLA Modules:
  0.0 422.3 jit_solution(12205356991977511797)
XLA Ops:
  7.2 4.4 %fusion.38 = (bf16[1,1,256,2048]{3,2,1,0:T(8,128)(2,1)}, bf16[1,1,256,2048]{3,2,1,0:T(8,128)(2,1)}, bf16[1,1,256,2048]{3,2,1,0:T(8,128)(2,1)}, bf16[1,1,256,2048]{3,2,1,0:T(8,128)(2,1)}) fusion(bf16[4,1,256,2048]{3,2,1,0:T(8,128)(2,1)} %param.22), kind=kLoop, calls=%fused_computation.82 | loop fusion | bytes 8388608 | tf_op jit(solution)/shard_map/slice | solution.py:133
  13.3 3.0 collective-permute-start
  16.3 17.5 %collective-permute-done = bf16[1,3,2,256,256]{4,3,2,1,0:T(8,128)(2,1)S(1)} collective-permute-done((bf16[1,3,2,256,256]{4,3,2,1,0:T(8,128)(2,1)S(1)}, bf16[1,3,2,256,256]{4,3,2,1,0:T(8,128)(2,1)S(1)}, u32[]{:S(2)}, u32[]{:S(2)}) %collective-permute-start) | collective-permute-done | bytes 786464 | tf_op jit(solution)/shard_map/ppermute | solution.py:129
  34.0 1.8 collective-permute-start.1
  35.8 34.0 %collective-permute-done.1 = bf16[2,3,2,256,256]{4,3,2,1,0:T(8,128)(2,1)S(1)} collective-permute-done((bf16[2,3,2,256,256]{4,3,2,1,0:T(8,128)(2,1)S(1)}, bf16[2,3,2,256,256]{4,3,2,1,0:T(8,128)(2,1)S(1)}, u32[]{:S(2)}, u32[]{:S(2)}) %collective-permute-start.1) | collective-permute-done | bytes 1572896 | tf_op jit(solution)/shard_map/ppermute | solution.py:129
  69.8 2.0 pad_maximum_fusion.1
  90.3 1.3 stack.46.info_ref
  92.2 2.1 stack.100.info_ref
  94.3 2.5 stack.104.info_ref
  99.7 5.1 %pad_maximum_fusion.refs_0_.refs_1_.refs_2_.refs_4_.refs_5_.refs_6_.refs_3_ = bf16[8,3,2,256,256]{4,3,2,1,0:T(8,128)(2,1)} fusion(bf16[4,3,2,256,256]{4,3,2,1,0:T(8,128)(2,1)} %collective-permute-done.2, bf16[2,3,2,256,256]{4,3,2,1,0:T(8,128)(2,1)S(1)} %collective-permute-done.1, bf16[1,3,2,256,256]{4,3,2,1,0:T(8,128)(2,1)S(1)} %collective-permute-done, ...), kind=kLoop, calls=%fused_computation | loop fusion | flops 9437184 | bytes 12582912 | tf_op jit(solution)/shard_map/concatenate | solution.py:137
  104.8 16.0 %fusion.17.dout_ref = bf16[256,2048]{1,0:T(8,128)(2,1)S(1)} fusion(bf16[2048,8192]{1,0:T(8,128)(2,1)} %param.23, bf16[1,1,256,8192]{3,2,1,0:T(8,128)(2,1)} %all-gather.15.cloned.1.call-done), kind=kOutput, calls=%fused_computation.13 | convolution fusion | flops 8590458880 | bytes 38797312 | tf_op jit(solution)/shard_map/dot_general | solution.py:160
  120.8 2.2 copy-done.4
  123.0 25.2 %attention_level.4 = (bf16[4,1,256,2048]{3,2,1,0:T(8,128)(2,1)}, f32[4,256,256]{2,1,0:T(8,128)S(1)}, f32[4,256,256]{2,1,0:T(8,128)S(1)}) custom-call(s32[8]{0:T(128)S(1)} %stack.104.info_ref, bf16[4,1,256,2048]{3,2,1,0:T(8,128)(2,1)S(1)} %copy-done.4, bf16[256,2048]{1,0:T(8,128)(2,1)S(1)} %fusion.17.dout_ref, ...), custom_call_target="tpu_custom_call" | custom-call | flops 21474836480 | bytes 3145728 | tf_op jit(solution)/shard_map/attention_level/pallas_call | solution.py:102
  148.2 0.8 fusion.39
  150.4 1.2 select_convert_fusion
  152.1 24.0 %all-gather.13.cloned.1.call-done = bf16[1,1,256,8192]{3,2,1,0:T(8,128)(2,1)} async-done(((bf16[1,1,256,2048]{3,2,1,0:T(8,128)(2,1)}), bf16[1,1,256,8192]{3,2,1,0:T(8,128)(2,1)}) %all-gather.13.cloned.1.call-update) | async-done | bytes 4194320 | tf_op jit(solution)/shard_map/all_gather | solution.py:133
  176.1 16.4 %fusion.14.dout_ref = bf16[256,2048]{1,0:T(8,128)(2,1)S(1)} fusion(bf16[2048,8192]{1,0:T(8,128)(2,1)} %param.23, bf16[1,1,256,8192]{3,2,1,0:T(8,128)(2,1)} %all-gather.13.cloned.1.call-done), kind=kOutput, calls=%fused_computation.12 | convolution fusion | flops 8590458880 | bytes 38797312 | tf_op jit(solution)/shard_map/dot_general | solution.py:160
  192.5 2.8 copy-done
  195.3 2.2 copy-done.5
  197.5 20.6 %attention_level.5 = (bf16[4,1,256,2048]{3,2,1,0:T(8,128)(2,1)}, f32[3,256,256]{2,1,0:T(8,128)S(1)}, f32[3,256,256]{2,1,0:T(8,128)S(1)}) custom-call(s32[8]{0:T(128)S(1)} %stack.100.info_ref, bf16[4,1,256,2048]{3,2,1,0:T(8,128)(2,1)S(1)} %copy-done.5, bf16[256,2048]{1,0:T(8,128)(2,1)S(1)} %fusion.14.dout_ref, ...), custom_call_target="tpu_custom_call", output_to_operand_aliasing={{0}: (9, {})} | custom-call | flops 16106127360 | bytes 3145728 | tf_op jit(solution)/shard_map/attention_level/pallas_call | solution.py:102
  218.2 0.8 fusion.41
  219.1 0.8 fusion.42
  220.0 1.4 add_convert_fusion
  221.4 35.6 %all-gather.11.cloned.1.call-done = bf16[1,1,256,8192]{3,2,1,0:T(8,128)(2,1)} async-done(((bf16[1,1,256,2048]{3,2,1,0:T(8,128)(2,1)}), bf16[1,1,256,8192]{3,2,1,0:T(8,128)(2,1)}) %all-gather.11.cloned.1.call-update) | async-done | bytes 4194320 | tf_op jit(solution)/shard_map/all_gather | solution.py:133
  257.0 16.4 %fusion.11.dout_ref = bf16[256,2048]{1,0:T(8,128)(2,1)S(1)} fusion(bf16[2048,8192]{1,0:T(8,128)(2,1)} %param.23, bf16[1,1,256,8192]{3,2,1,0:T(8,128)(2,1)} %all-gather.11.cloned.1.call-done), kind=kOutput, calls=%fused_computation.11 | convolution fusion | flops 8590458880 | bytes 38797312 | tf_op jit(solution)/shard_map/dot_general | solution.py:160
  273.4 2.8 copy-done.1
  276.2 2.2 copy-done.6
  278.4 16.2 %attention_level.6 = (bf16[4,1,256,2048]{3,2,1,0:T(8,128)(2,1)}, f32[2,256,256]{2,1,0:T(8,128)S(1)}, f32[2,256,256]{2,1,0:T(8,128)S(1)}) custom-call(s32[8]{0:T(128)S(1)} %stack.46.info_ref, bf16[4,1,256,2048]{3,2,1,0:T(8,128)(2,1)S(1)} %copy-done.6, bf16[256,2048]{1,0:T(8,128)(2,1)S(1)} %fusion.11.dout_ref, ...), custom_call_target="tpu_custom_call", output_to_operand_aliasing={{0}: (7, {})} | custom-call | flops 10737418240 | bytes 3145728 | tf_op jit(solution)/shard_map/attention_level/pallas_call | solution.py:102
  295.5 0.8 fusion.44
  296.4 1.5 add_convert_fusion.1
  297.8 40.0 %all-gather.9.cloned.1.call-done = bf16[1,1,256,8192]{3,2,1,0:T(8,128)(2,1)} async-done(((bf16[1,1,256,2048]{3,2,1,0:T(8,128)(2,1)}), bf16[1,1,256,8192]{3,2,1,0:T(8,128)(2,1)}) %all-gather.9.cloned.1.call-update) | async-done | bytes 4194320 | tf_op jit(solution)/shard_map/all_gather | solution.py:133
  337.8 15.7 %fusion.8.dout_ref = bf16[256,2048]{1,0:T(8,128)(2,1)S(1)} fusion(bf16[2048,8192]{1,0:T(8,128)(2,1)} %param.23, bf16[1,1,256,8192]{3,2,1,0:T(8,128)(2,1)} %all-gather.9.cloned.1.call-done), kind=kOutput, calls=%fused_computation.10 | convolution fusion | flops 8590458880 | bytes 38797312 | tf_op jit(solution)/shard_map/dot_general | solution.py:160
  353.5 2.2 copy-done.7
  355.7 12.7 %attention_level.7 = (bf16[4,1,256,2048]{3,2,1,0:T(8,128)(2,1)}, f32[1,256,256]{2,1,0:T(8,128)S(1)}, f32[1,256,256]{2,1,0:T(8,128)S(1)}) custom-call(s32[8]{0:T(128)S(1)} %stack.44.info_ref, bf16[4,1,256,2048]{3,2,1,0:T(8,128)(2,1)S(1)} %copy-done.7, bf16[256,2048]{1,0:T(8,128)(2,1)S(1)} %fusion.8.dout_ref, ...), custom_call_target="tpu_custom_call", output_to_operand_aliasing={{0}: (5, {})} | custom-call | flops 5368709120 | bytes 3145728 | tf_op jit(solution)/shard_map/attention_level/pallas_call | solution.py:102
  368.4 1.8 fusion.37
  370.3 1.5 collective-permute-start.7
  371.8 1.8 fusion.36
  374.3 1.6 convert_add_fusion
  376.0 1.5 collective-permute-start.10
  377.5 7.6 %collective-permute-done.7 = bf16[2,2,256,256]{3,2,1,0:T(8,128)(2,1)S(1)} collective-permute-done((bf16[2,2,256,256]{3,2,1,0:T(8,128)(2,1)S(1)}, bf16[2,2,256,256]{3,2,1,0:T(8,128)(2,1)S(1)}, u32[]{:S(2)}, u32[]{:S(2)}) %collective-permute-start.7) | collective-permute-done | bytes 524320 | tf_op jit(solution)/shard_map/ppermute | solution.py:129
  385.3 1.5 collective-permute-start.8
  386.9 9.5 %collective-permute-done.4 = bf16[2,2,256,256]{3,2,1,0:T(8,128)(2,1)S(1)} collective-permute-done((bf16[2,2,256,256]{3,2,1,0:T(8,128)(2,1)S(1)}, bf16[2,2,256,256]{3,2,1,0:T(8,128)(2,1)S(1)}, u32[]{:S(2)}, u32[]{:S(2)}) %collective-permute-start.4) | collective-permute-done | bytes 524320 | tf_op jit(solution)/shard_map/ppermute | solution.py:129
  396.6 1.5 collective-permute-start.5
  398.1 8.3 %collective-permute-done.10 = bf16[2,2,256,256]{3,2,1,0:T(8,128)(2,1)S(1)} collective-permute-done((bf16[2,2,256,256]{3,2,1,0:T(8,128)(2,1)S(1)}, bf16[2,2,256,256]{3,2,1,0:T(8,128)(2,1)S(1)}, u32[]{:S(2)}, u32[]{:S(2)}) %collective-permute-start.10) | collective-permute-done | bytes 524320 | tf_op jit(solution)/shard_map/ppermute | solution.py:129
  406.7 1.5 collective-permute-start.11
  408.5 5.4 %collective-permute-done.11 = bf16[1,2,256,256]{3,2,1,0:T(8,128)(2,1)S(1)} collective-permute-done((bf16[1,2,256,256]{3,2,1,0:T(8,128)(2,1)S(1)}, bf16[1,2,256,256]{3,2,1,0:T(8,128)(2,1)S(1)}, u32[]{:S(2)}, u32[]{:S(2)}) %collective-permute-start.11) | collective-permute-done | bytes 262176 | tf_op jit(solution)/shard_map/ppermute | solution.py:129
  414.0 0.9 maximum_bitcast_fusion.2
  414.9 0.9 maximum_bitcast_fusion.1
  (135 shorter events, 13.2 us)
Async XLA Ops:
  7.2 97.6 %all-gather.15.cloned.1.call-start = ((), (), s32[]{:S(2)}) async-start(), calls=%async_computation.3 | async-start | bytes 5242880 | tf_op jit(solution)/shard_map/all_gather | solution.py:133
  11.6 164.5 %all-gather.13.cloned.1.call-start = ((), (), s32[]{:S(2)}) async-start(), calls=%async_computation.2 | async-start | bytes 5242880 | tf_op jit(solution)/shard_map/all_gather | solution.py:133
  12.4 244.6 %all-gather.11.cloned.1.call-start = ((), (), s32[]{:S(2)}) async-start(), calls=%async_computation.1 | async-start | bytes 5242880 | tf_op jit(solution)/shard_map/all_gather | solution.py:133
  13.1 324.7 %all-gather.9.cloned.1.call-start = ((), (), s32[]{:S(2)}) async-start(), calls=%async_computation | async-start | bytes 5242880 | tf_op jit(solution)/shard_map/all_gather | solution.py:133
  13.3 20.6 %collective-permute-start = (bf16[1,3,2,256,256]{4,3,2,1,0:T(8,128)(2,1)S(1)}, bf16[1,3,2,256,256]{4,3,2,1,0:T(8,128)(2,1)S(1)}, u32[]{:S(2)}, u32[]{:S(2)}) collective-permute-start(bf16[1,3,2,256,256]{4,3,2,1,0:T(8,128)(2,1)S(1)} %maximum_bitcast_fusion), channel_id=1, source_target_pairs={{0,16},{4,20},{8,24},{12,28},{16,0},{20,4},{24,8},{28,12},{1,17},{... | collective-permute-start | bytes 2359304 | tf_op jit(solution)/shard_map/ppermute | solution.py:129
  34.0 37.8 %copy-start.34 = (s32[3,8]{1,0:T(4,128)S(1)}, s32[3,8]{1,0:T(4,128)}, u32[]{:S(2)}) copy-start(s32[3,8]{1,0:T(4,128)} %param.24) | copy-start | bytes 292
  34.0 54.8 %copy-start.28 = (s32[4,8]{1,0:T(4,128)S(1)}, s32[4,8]{1,0:T(4,128)}, u32[]{:S(2)}) copy-start(s32[4,8]{1,0:T(4,128)} %param.25) | copy-start | bytes 388
  34.0 65.1 %copy-start.37 = (s32[4]{0:T(128)S(1)}, s32[4]{0:T(128)}, u32[]{:S(2)}) copy-start(s32[4]{0:T(128)} %constant.86.clone) | copy-start | bytes 52
  34.0 35.8 %collective-permute-start.1 = (bf16[2,3,2,256,256]{4,3,2,1,0:T(8,128)(2,1)S(1)}, bf16[2,3,2,256,256]{4,3,2,1,0:T(8,128)(2,1)S(1)}, u32[]{:S(2)}, u32[]{:S(2)}) collective-permute-start(bf16[2,3,2,256,256]{4,3,2,1,0:T(8,128)(2,1)S(1)} %pad_maximum_fusion.2), channel_id=1, source_target_pairs={{0,8},{4,12},{8,0},{12,4},{16,24},{20,28},{24,16},{28,20},{1,9},{5... | collective-permute-start | bytes 4718600 | tf_op jit(solution)/shard_map/ppermute | solution.py:129
  71.8 27.9 %collective-permute-start.2 = (bf16[4,3,2,256,256]{4,3,2,1,0:T(8,128)(2,1)}, bf16[4,3,2,256,256]{4,3,2,1,0:T(8,128)(2,1)}, u32[]{:S(2)}, u32[]{:S(2)}) collective-permute-start(bf16[4,3,2,256,256]{4,3,2,1,0:T(8,128)(2,1)} %pad_maximum_fusion.1), channel_id=1, source_target_pairs={{0,4},{4,0},{8,12},{12,8},{16,20},{20,16},{24,28},{28,24},{1,5},{5... | collective-permute-start | bytes 9437192 | tf_op jit(solution)/shard_map/ppermute | solution.py:129
  104.8 16.0 %copy-start.2 = (bf16[4,1,256,256]{3,2,1,0:T(8,128)(2,1)S(1)}, bf16[4,1,256,256]{3,2,1,0:T(8,128)(2,1)}, u32[]{:S(2)}) copy-start(bf16[4,1,256,256]{3,2,1,0:T(8,128)(2,1)} %refs_0_.1) | copy-start | bytes 1572868
  104.8 16.0 %copy-start.3 = (bf16[4,1,256,256]{3,2,1,0:T(8,128)(2,1)S(1)}, bf16[4,1,256,256]{3,2,1,0:T(8,128)(2,1)}, u32[]{:S(2)}) copy-start(bf16[4,1,256,256]{3,2,1,0:T(8,128)(2,1)} %refs_1_.3) | copy-start | bytes 1572868
  120.8 2.2 copy-start.4
  148.2 2.2 copy-start.27
  151.7 222.7 %collective-permute-start.9 = (bf16[4,2,256,256]{3,2,1,0:T(8,128)(2,1)}, bf16[4,2,256,256]{3,2,1,0:T(8,128)(2,1)}, u32[]{:S(2)}, u32[]{:S(2)}) collective-permute-start(bf16[4,2,256,256]{3,2,1,0:T(8,128)(2,1)} %select_convert_fusion), channel_id=1, source_target_pairs={{0,4},{4,0},{8,12},{12,8},{16,20},{20,16},{24,28},{28,24},{1,5},{5... | collective-permute-start | bytes 3145736 | tf_op jit(solution)/shard_map/ppermute | solution.py:129
  192.5 2.8 copy-start
  195.3 2.2 copy-start.5
  218.2 1.8 copy-start.12
  218.2 1.8 copy-start.32
  218.2 1.8 copy-start.33
  219.1 2.3 copy-start.19
  219.1 2.3 copy-start.20
  221.4 147.0 %collective-permute-start.6 = (bf16[4,2,256,256]{3,2,1,0:T(8,128)(2,1)}, bf16[4,2,256,256]{3,2,1,0:T(8,128)(2,1)}, u32[]{:S(2)}, u32[]{:S(2)}) collective-permute-start(bf16[4,2,256,256]{3,2,1,0:T(8,128)(2,1)} %add_convert_fusion), channel_id=1, source_target_pairs={{0,4},{4,0},{8,12},{12,8},{16,20},{20,16},{24,28},{28,24},{1,5},{5... | collective-permute-start | bytes 3145736 | tf_op jit(solution)/shard_map/ppermute | solution.py:129
  273.4 2.8 copy-start.1
  276.2 2.2 copy-start.6
  294.7 1.6 copy-start.30
  294.7 1.7 copy-start.31
  297.8 74.0 %collective-permute-start.3 = (bf16[4,2,256,256]{3,2,1,0:T(8,128)(2,1)}, bf16[4,2,256,256]{3,2,1,0:T(8,128)(2,1)}, u32[]{:S(2)}, u32[]{:S(2)}) collective-permute-start(bf16[4,2,256,256]{3,2,1,0:T(8,128)(2,1)} %add_convert_fusion.1), channel_id=1, source_target_pairs={{0,4},{4,0},{8,12},{12,8},{16,20},{20,16},{24,28},{28,24},{1,5},{5... | collective-permute-start | bytes 3145736 | tf_op jit(solution)/shard_map/ppermute | solution.py:129
  353.5 2.2 copy-start.7
  355.7 12.7 %copy-start.13 = (f32[2,256,256]{2,1,0:T(8,128)S(1)}, f32[2,256,256]{2,1,0:T(8,128)}, u32[]{:S(2)}) copy-start(f32[2,256,256]{2,1,0:T(8,128)} %copy-done.12) | copy-start | bytes 1572868
  355.7 12.7 %copy-start.15 = (f32[2,256,256]{2,1,0:T(8,128)S(1)}, f32[2,256,256]{2,1,0:T(8,128)}, u32[]{:S(2)}) copy-start(f32[2,256,256]{2,1,0:T(8,128)} %copy-done.14) | copy-start | bytes 1572868
  355.7 12.7 %copy-start.25 = (pred[4]{0:T(512)(128)(4,1)S(1)}, pred[4]{0:T(512)(128)(4,1)}, u32[]{:S(2)}) copy-start(pred[4]{0:T(512)(128)(4,1)} %get-tuple-element.94) | copy-start | bytes 16
  355.7 12.7 %copy-start.26 = (pred[4]{0:T(512)(128)(4,1)S(1)}, pred[4]{0:T(512)(128)(4,1)}, u32[]{:S(2)}) copy-start(pred[4]{0:T(512)(128)(4,1)} %get-tuple-element.95) | copy-start | bytes 16
  368.4 3.4 copy-start.9
  368.4 3.4 copy-start.11
  368.4 3.4 copy-start.24
  368.4 3.4 copy-start.36
  370.3 14.9 %collective-permute-start.7 = (bf16[2,2,256,256]{3,2,1,0:T(8,128)(2,1)S(1)}, bf16[2,2,256,256]{3,2,1,0:T(8,128)(2,1)S(1)}, u32[]{:S(2)}, u32[]{:S(2)}) collective-permute-start(bf16[2,2,256,256]{3,2,1,0:T(8,128)(2,1)S(1)} %slice.207), channel_id=1, source_target_pairs={{0,8},{4,12},{8,0},{12,4},{16,24},{20,28},{24,16},{28,20},{1,9},{5... | collective-permute-start | bytes 1572872 | tf_op jit(solution)/shard_map/ppermute | solution.py:129
  371.8 2.5 copy-start.35
  373.7 22.7 %collective-permute-start.4 = (bf16[2,2,256,256]{3,2,1,0:T(8,128)(2,1)S(1)}, bf16[2,2,256,256]{3,2,1,0:T(8,128)(2,1)S(1)}, u32[]{:S(2)}, u32[]{:S(2)}) collective-permute-start(bf16[2,2,256,256]{3,2,1,0:T(8,128)(2,1)S(1)} %slice.196), channel_id=1, source_target_pairs={{0,8},{4,12},{8,0},{12,4},{16,24},{20,28},{24,16},{28,20},{1,9},{5... | collective-permute-start | bytes 1572872 | tf_op jit(solution)/shard_map/ppermute | solution.py:129
  376.0 30.5 %collective-permute-start.10 = (bf16[2,2,256,256]{3,2,1,0:T(8,128)(2,1)S(1)}, bf16[2,2,256,256]{3,2,1,0:T(8,128)(2,1)S(1)}, u32[]{:S(2)}, u32[]{:S(2)}) collective-permute-start(bf16[2,2,256,256]{3,2,1,0:T(8,128)(2,1)S(1)} %slice.216), channel_id=1, source_target_pairs={{0,8},{4,12},{8,0},{12,4},{16,24},{20,28},{24,16},{28,20},{1,9},{5... | collective-permute-start | bytes 1572872 | tf_op jit(solution)/shard_map/ppermute | solution.py:129
  385.3 22.9 %collective-permute-start.8 = (bf16[1,2,256,256]{3,2,1,0:T(8,128)(2,1)S(1)}, bf16[1,2,256,256]{3,2,1,0:T(8,128)(2,1)S(1)}, u32[]{:S(2)}, u32[]{:S(2)}) collective-permute-start(bf16[1,2,256,256]{3,2,1,0:T(8,128)(2,1)S(1)} %slice.269), channel_id=1, source_target_pairs={{0,16},{4,20},{8,24},{12,28},{16,0},{20,4},{24,8},{28,12},{1,17},{... | collective-permute-start | bytes 786440 | tf_op jit(solution)/shard_map/ppermute | solution.py:129
  396.5 11.7 %copy-start.17 = (f32[1,256,256]{2,1,0:T(8,128)S(1)}, f32[1,256,256]{2,1,0:T(8,128)}, u32[]{:S(2)}) copy-start(f32[1,256,256]{2,1,0:T(8,128)} %get-tuple-element.53) | copy-start | bytes 786436
  396.5 11.7 %copy-start.18 = (f32[1,256,256]{2,1,0:T(8,128)S(1)}, f32[1,256,256]{2,1,0:T(8,128)}, u32[]{:S(2)}) copy-start(f32[1,256,256]{2,1,0:T(8,128)} %get-tuple-element.55) | copy-start | bytes 786436
  396.6 11.8 %collective-permute-start.5 = (bf16[1,2,256,256]{3,2,1,0:T(8,128)(2,1)S(1)}, bf16[1,2,256,256]{3,2,1,0:T(8,128)(2,1)S(1)}, u32[]{:S(2)}, u32[]{:S(2)}) collective-permute-start(bf16[1,2,256,256]{3,2,1,0:T(8,128)(2,1)S(1)} %slice.270), channel_id=1, source_target_pairs={{0,16},{4,20},{8,24},{12,28},{16,0},{20,4},{24,8},{28,12},{1,17},{... | collective-permute-start | bytes 786440 | tf_op jit(solution)/shard_map/ppermute | solution.py:129
  406.7 7.2 %collective-permute-start.11 = (bf16[1,2,256,256]{3,2,1,0:T(8,128)(2,1)S(1)}, bf16[1,2,256,256]{3,2,1,0:T(8,128)(2,1)S(1)}, u32[]{:S(2)}, u32[]{:S(2)}) collective-permute-start(bf16[1,2,256,256]{3,2,1,0:T(8,128)(2,1)S(1)} %slice.268), channel_id=1, source_target_pairs={{0,16},{4,20},{8,24},{12,28},{16,0},{20,4},{24,8},{28,12},{1,17},{... | collective-permute-start | bytes 786440 | tf_op jit(solution)/shard_map/ppermute | solution.py:129
  408.2 5.7 %copy-start.16 = (f32[1,256,256]{2,1,0:T(8,128)S(1)}, f32[1,256,256]{2,1,0:T(8,128)}, u32[]{:S(2)}) copy-start(f32[1,256,256]{2,1,0:T(8,128)} %get-tuple-element.50) | copy-start | bytes 786436
  408.4 5.7 %copy-start.23 = (bf16[1,256,256]{2,1,0:T(8,128)(2,1)S(1)}, bf16[1,256,256]{2,1,0:T(8,128)(2,1)}, u32[]{:S(2)}) copy-start(bf16[1,256,256]{2,1,0:T(8,128)(2,1)} %slice.271) | copy-start | bytes 393220
  (8 other events, 12.5 us)
Sparse Core Ops, SparseCore 0:
  11.7 83.4 all-gather.14
  96.8 79.2 all-gather.12
  177.7 79.2 all-gather.10
  258.5 79.2 all-gather.8

commit v2 on v1

v2 whole, which is shorter than its diff:
```python
import functools

import jax
import jax.numpy as jnp
from jax import lax
from jax.experimental import pallas as pl
from jax.experimental.pallas import tpu as pltpu
from jax.sharding import PartitionSpec as P

HD = 128
MASKED = -1e30
NT = (((1,), (1,)), ((), ()))
NN = (((1,), (0,)), ((), ()))
TN = (((0,), (0,)), ((), ()))


def pick_row(table, index_value):
    return lax.dynamic_index_in_dim(table, index_value, 0, keepdims=False)


def attention_kernel(level, has_base, info_ref, q_ref, cot_ref, weight_ref, *refs):
    blocks = level + 1
    key_refs, value_refs = refs[:blocks], refs[blocks : 2 * blocks]
    dq_ref, dk_ref, dv_ref = refs[2 * blocks + has_base :]
    seg = cot_ref.shape[0]
    heads = weight_ref.shape[0] // HD
    scale = 1.0 / HD**0.5
    own_len = info_ref[4 + level]
    keys = [ref[...].reshape(seg, HD) for ref in key_refs]
    values = [ref[...].reshape(seg, HD) for ref in value_refs]
    key_pos = lax.broadcasted_iota(jnp.int32, (seg, seg), 0)
    query_pos = lax.broadcasted_iota(jnp.int32, (seg, seg), 1)

    def dot(a, b, dims):
        return lax.dot_general(a, b, dims, preferred_element_type=jnp.float32)

    @pl.when(pl.program_id(1) == 0)
    def _():
        dk_ref[...] = jnp.zeros_like(dk_ref)
        dv_ref[...] = jnp.zeros_like(dv_ref)

    douts = dot(cot_ref[...], weight_ref[...], NT).astype(jnp.bfloat16)
    row = lax.broadcasted_iota(jnp.int32, douts.shape, 0)
    douts = jnp.where(row < own_len, douts, jnp.zeros_like(douts))
    for h in range(heads):
        columns = slice(h * HD, (h + 1) * HD)
        q = q_ref[0, 0, :, columns]
        dout = douts[:, columns]
        scores = []
        for m in range(blocks):
            allowed = key_pos < info_ref[4 + m]
            if m == level:
                allowed = allowed & (key_pos <= query_pos)
            scores.append(jnp.where(allowed, dot(keys[m], q, NT) * scale, MASKED))
        top = functools.reduce(jnp.maximum, [jnp.max(s, axis=0, keepdims=True) for s in scores])
        exps = [jnp.exp(s - top) for s in scores]
        total = functools.reduce(jnp.add, [jnp.sum(e, axis=0, keepdims=True) for e in exps])
        inverse = 1.0 / total
        probs = [e * inverse for e in exps]
        narrow = [p.astype(jnp.bfloat16) for p in probs]
        dprobs = [dot(v, dout, NT) for v in values]
        delta = functools.reduce(
            jnp.add,
            [
                jnp.sum(pb.astype(jnp.float32) * dp, axis=0, keepdims=True)
                for pb, dp in zip(narrow, dprobs)
            ],
        )
        dq = jnp.zeros((HD, seg), jnp.float32)
        for m in range(blocks):
            ds = (probs[m] * (dprobs[m] - delta)).astype(jnp.bfloat16)
            dk_ref[m] += dot(ds, q, NN) * scale
            dv_ref[m] += dot(narrow[m], dout, NN)
            dq = dq + dot(keys[m], ds, TN)
        dq_ref[0, 0, :, columns] = (dq * scale).T.astype(jnp.bfloat16)


def attention_level(level, info, queries, cot, weight, key_rows, value_rows, kv_all, base):
    levels, _, seg, q_width = queries.shape
    kv_width = key_rows.shape[3]
    kv_local = kv_width // HD
    group = q_width // kv_width
    blocks = level + 1
    heads = 2
    steps = group // heads
    model = weight.shape[1]

    def gathered(kind, m):
        return pl.BlockSpec(
            (1, 1, 1, seg, HD), lambda n, g, info, m=m, k=kind: (info[m], m, k, 0, n)
        )

    q_spec = pl.BlockSpec(
        (1, 1, seg, heads * HD), lambda n, g, info: (level, 0, 0, n * steps + g)
    )
    own_spec = pl.BlockSpec((1, 1, seg, HD), lambda n, g, info: (level, 0, 0, n))
    cot_spec = pl.BlockSpec((seg, model), lambda n, g, info: (0, 0))
    weight_spec = pl.BlockSpec((heads * HD, model), lambda n, g, info: (n * steps + g, 0))
    grad_spec = pl.BlockSpec((blocks, seg, HD), lambda n, g, info: (0, 0, n))
    in_specs = [q_spec, cot_spec, weight_spec]
    in_specs += [gathered(0, m) for m in range(level)] + [own_spec]
    in_specs += [gathered(1, m) for m in range(level)] + [own_spec]
    operands = [queries, cot, weight]
    operands += [kv_all] * level + [key_rows] + [kv_all] * level + [value_rows]
    aliases = {}
    if base is not None:
        in_specs.append(pl.BlockSpec(memory_space=pl.ANY))
        operands.append(base)
        aliases = {len(operands): 0}
    grad_shape = jax.ShapeDtypeStruct((blocks, seg, kv_width), jnp.float32)
    products = 5 * 2 * seg * seg * HD * blocks * kv_local * group
    return pl.pallas_call(
        functools.partial(attention_kernel, level, int(base is not None)),
        grid_spec=pltpu.PrefetchScalarGridSpec(
            num_scalar_prefetch=1,
            grid=(kv_local, steps),
            in_specs=in_specs,
            out_specs=[q_spec, grad_spec, grad_spec],
        ),
        out_shape=[jax.ShapeDtypeStruct(queries.shape, jnp.bfloat16), grad_shape, grad_shape],
        input_output_aliases=aliases,
        compiler_params=pltpu.CompilerParams(vmem_limit_bytes=48 * 1024 * 1024),
        cost_estimate=pl.CostEstimate(
            flops=4 * products + 2 * seg * model * q_width,
            bytes_accessed=3 * seg * q_width * 2 + q_width * model * 2,
            transcendentals=seg * seg * blocks * kv_local * group,
        ),
        name="attention_level",
    )(info, *operands)


def local(node_count, head_count, queries, key_rows, value_rows, cotangent, out_weight, parents, seg_len):
    levels, _, seg, q_width = queries.shape
    bits = node_count.bit_length() - 1
    me = lax.axis_index("branch")

    def swap(array, bit):
        pairs = [(i, i ^ (1 << bit)) for i in range(node_count)]
        return lax.ppermute(array, "branch", pairs)

    line_level = 1
    place = lax.axis_index("head")
    width = cotangent.shape[3]
    gathered = [None] * levels
    for level in reversed(range(levels)):
        if level != line_level:
            gathered[level] = lax.all_gather(cotangent[level, 0], "head", axis=1, tiled=True)
    line = cotangent[line_level, 0]
    uphill = [line]
    downhill = [line]

    def hop():
        done = len(uphill)
        up = [(i, i + 1) for i in range(done - 1, head_count - 1)]
        down = [(i + 1, i) for i in range(head_count - done)]
        uphill.append(lax.ppermute(uphill[-1], "head", up))
        downhill.append(lax.ppermute(downhill[-1], "head", down))

    kv_all = jnp.stack([key_rows[: levels - 1, 0], value_rows[: levels - 1, 0]], axis=1)[None]
    for bit in reversed(range(bits)):
        kv_all = jnp.concatenate([kv_all, swap(kv_all, bit)], axis=0)

    offsets = []
    infos = []
    for level in range(levels):
        lineage = [None] * (level + 1)
        lineage[level] = me
        for m in reversed(range(level)):
            lineage[m] = pick_row(parents[m], lineage[m + 1])
        relative = [node ^ me for node in lineage]
        slots = [
            sum(((r >> b) & 1) << (bits - 1 - b) for b in range(bits)) for r in relative
        ]
        lengths = [pick_row(seg_len[m], lineage[m]) for m in range(level + 1)]
        pad = [jnp.int32(0)] * (levels - 1 - level)
        infos.append(jnp.stack(slots + pad + lengths + pad).astype(jnp.int32))
        offsets.append(relative)

    key_terms = [[] for _ in range(levels)]
    received = [None] * levels
    key_grads = [None] * levels
    value_grads = [None] * levels
    query_grad = None
    for level in reversed(range(levels)):
        if level == line_level:
            while len(uphill) < head_count:
                hop()
            whole = jnp.zeros((seg, head_count * width), cotangent.dtype)
            whole = lax.dynamic_update_slice(whole, line, (0, place * width))
            for j in range(1, head_count):
                ahead = place + j < head_count
                piece = jnp.where(ahead, downhill[j], uphill[head_count - j])
                at = lax.rem(place + j, head_count) * width
                whole = lax.dynamic_update_slice(whole, piece, (0, at))
            gathered[level] = whole
        elif level > line_level and len(uphill) < head_count:
            hop()
            gathered[level], uphill[-1], downhill[-1] = lax.optimization_barrier(
                (gathered[level], uphill[-1], downhill[-1])
            )
        if level <= line_level:
            due = range(level + 1 if level else 0, levels - 1)
            for m in due:
                gathered[level], received[m] = lax.optimization_barrier(
                    (gathered[level], received[m])
                )
        query_grad, dk, dv = attention_level(
            level, infos[level], queries, gathered[level], out_weight,
            key_rows, value_rows, kv_all, query_grad,
        )
        own = jnp.stack([dk[level], dv[level]])
        if level < levels - 1:
            own = own + received[level]
        key_grads[level] = own[0].astype(jnp.bfloat16)
        value_grads[level] = own[1].astype(jnp.bfloat16)
        for m in range(level):
            key_terms[m].append((offsets[level][m], dk[m], dv[m]))
        if level > 0:
            m = level - 1

            def spread(ids):
                total = jnp.zeros((len(ids), 2, seg, key_rows.shape[3]), jnp.float32)
                for offset, dk_term, dv_term in key_terms[m]:
                    hit = (jnp.array(ids, jnp.int32) == offset)[:, None, None, None]
                    total = total + jnp.where(hit, jnp.stack([dk_term, dv_term])[None], 0.0)
                return total

            keep = spread(range(0, node_count, 2))
            send = spread(range(1, node_count, 2)).astype(jnp.bfloat16)
            for bit in range(bits):
                held = keep + swap(send, bit).astype(jnp.float32)
                if bit + 1 < bits:
                    keep = held[0::2]
                    send = held[1::2].astype(jnp.bfloat16)
            received[m] = held[0]
    key_grad = jnp.stack(key_grads)[:, None]
    value_grad = jnp.stack(value_grads)[:, None]
    return query_grad, key_grad, value_grad


def solution(mesh):
    wide = P(None, "branch", None, "head")
    in_specs = (wide, wide, wide, wide, P("head", None), P(), P())
    return jax.shard_map(
        functools.partial(local, mesh.shape["branch"], mesh.shape["head"]),
        mesh=mesh,
        in_specs=in_specs,
        out_specs=(wide, wide, wide),
        check_vma=False,
    )
```

time: 423 us -> 425 us (level)
  Pallas kernels: 74.7 us -> 149 us
  matrix products: 64.4 us -> 0 us
  waiting for transfers between devices: 183 us -> 166 us
  starting transfers between devices: 13.8 us -> 24 us
  local copies, waits for them, and re-layouts: 34.3 us -> 26.5 us
  other arithmetic: 22.1 us -> 28.6 us
    pallas_call x4, Pallas kernels: 74.7 us -> 149 us  [attention_level(): pl.pallas_call(functools.partial(attention_kernel, level, int(base is not...]
    all_gather x4 -> x3, waiting for transfers between devices: 99.5 us -> 32.6 us  [local(): lax.all_gather(cotangent[level, 0], 'head', axis=1, tiled=True)]
    dot_general x4 -> x0, matrix products: 64.4 us -> none  [local(): lax.dot_general(gathered[level], out_weight, NT, preferred_element_type=j...]
    ppermute x0 -> x6, waiting for transfers between devices: none -> 52.5 us  [the longest x3 43.2 us: hop(): downhill.append(lax.ppermute(downhill[-1], 'head', down))]
    unnamed x76 -> x42, local copies, waits for them, and re-layouts: 14.6 us -> 3.06 us
    ppermute x0 -> x6, starting transfers between devices: none -> 10.8 us  [the longest x3 6.94 us: hop(): uphill.append(lax.ppermute(uphill[-1], 'head', up))]
    dynamic_update_slice x0 -> x3, other arithmetic: none -> 6.58 us  [local(): whole = lax.dynamic_update_slice(whole, piece, (0, at))]
  transfers between devices with their start and end apart: 16 -> 21, of which waited for: 9 -> 10; matrix products, arithmetic and copies ran while one was open for 24% -> 11% of each run, Pallas kernels for 18% -> 29%
where the time goes in v2:
time: 425 us; the launch traced here: 424 us
  waiting for transfers between devices  166 us (39%)
  Pallas kernels  149 us (35%)
  between operations  29.7 us (7%)
  other arithmetic  28.6 us (7%)
  local copies, waits for them, and re-layouts  26.5 us (6%)
  starting transfers between devices  24 us (6%)
    pallas_call x4, Pallas kernels, attention_level(): pl.pallas_call(functools.partial(attention_kernel, level, int(base is not...  149 us
    ppermute x12, waiting for transfers between devices, swap(): return lax.ppermute(array, 'branch', pairs)  81 us
    ppermute x3, waiting for transfers between devices, hop(): downhill.append(lax.ppermute(downhill[-1], 'head', down))  43.2 us
    all_gather x3, waiting for transfers between devices, local(): lax.all_gather(cotangent[level, 0], 'head', axis=1, tiled=True)  32.6 us
    ppermute x12, starting transfers between devices, swap(): return lax.ppermute(array, 'branch', pairs)  13.1 us
    ppermute x3, waiting for transfers between devices, hop(): uphill.append(lax.ppermute(uphill[-1], 'head', up))  9.35 us
  transfers between devices with their start and end apart: 21, of which 10 were waited for; matrix products, arithmetic and copies ran while one was open for 11% of the time, Pallas kernels for 29%

profile of v2, /device:TPU:0, one launch (start us, length us, event | category | flops | bytes accessed | tf_op | source)
XLA Modules:
  0.0 424.3 jit_solution(3570612634222245116)
XLA Ops:
  7.2 4.4 %fusion.17 = (bf16[1,1,256,2048]{3,2,1,0:T(8,128)(2,1)}, bf16[1,1,256,2048]{3,2,1,0:T(8,128)(2,1)}, bf16[1,1,256,2048]{3,2,1,0:T(8,128)(2,1)}, bf16[256,2048]{1,0:T(8,128)(2,1)}) fusion(bf16[4,1,256,2048]{3,2,1,0:T(8,128)(2,1)} %param.22), kind=kLoop, calls=%fused_computation.75 | loop fusion | bytes 8388608 | tf_op jit(solution)/shard_map/slice | solution.py:147
  11.6 0.9 slice-done
  12.8 3.0 collective-permute-start.2
  15.8 17.5 %collective-permute-done.2 = bf16[1,3,2,256,256]{4,3,2,1,0:T(8,128)(2,1)S(1)} collective-permute-done((bf16[1,3,2,256,256]{4,3,2,1,0:T(8,128)(2,1)S(1)}, bf16[1,3,2,256,256]{4,3,2,1,0:T(8,128)(2,1)S(1)}, u32[]{:S(2)}, u32[]{:S(2)}) %collective-permute-start.2) | collective-permute-done | bytes 786464 | tf_op jit(solution)/shard_map/ppermute | solution.py:139
  33.5 1.8 collective-permute-start.3
  35.3 34.0 %collective-permute-done.3 = bf16[2,3,2,256,256]{4,3,2,1,0:T(8,128)(2,1)S(1)} collective-permute-done((bf16[2,3,2,256,256]{4,3,2,1,0:T(8,128)(2,1)S(1)}, bf16[2,3,2,256,256]{4,3,2,1,0:T(8,128)(2,1)S(1)}, u32[]{:S(2)}, u32[]{:S(2)}) %collective-permute-start.3) | collective-permute-done | bytes 1572896 | tf_op jit(solution)/shard_map/ppermute | solution.py:139
  69.3 2.2 pad_maximum_fusion.1
  71.5 4.4 %collective-permute-start = (bf16[256,2048]{1,0:T(8,128)(2,1)}, bf16[256,2048]{1,0:T(8,128)(2,1)}, u32[]{:S(2)}, u32[]{:S(2)}) collective-permute-start(bf16[256,2048]{1,0:T(8,128)(2,1)} %get-tuple-element.61), channel_id=1, source_target_pairs={{0,1},{1,2},{2,3},{4,5},{5,6},{6,7},{8,9},{9,10},{10,11},{12,13},{... | collective-permute-start | bytes 3145736 | tf_op jit(solution)/shard_map/ppermute | solution.py:156
  75.9 1.3 collective-permute-start.1
  95.8 2.6 stack.48.info_ref
  98.5 5.8 %pad_maximum_fusion.refs_0_.refs_1_.refs_2_.refs_4_.refs_5_.refs_6_.refs_3_ = bf16[8,3,2,256,256]{4,3,2,1,0:T(8,128)(2,1)} fusion(bf16[4,3,2,256,256]{4,3,2,1,0:T(8,128)(2,1)} %collective-permute-done.4, bf16[2,3,2,256,256]{4,3,2,1,0:T(8,128)(2,1)} %copy-done.3, bf16[1,3,2,256,256]{4,3,2,1,0:T(8,128)(2,1)S(1)} %collective-permute-done.2, ...), kind=kLoop, calls=%fused_computation | loop fusion | flops 9437184 | bytes 12582912 | tf_op jit(solution)/shard_map/concatenate | solution.py:161
  104.3 9.3 %collective-permute-done = bf16[256,2048]{1,0:T(8,128)(2,1)} collective-permute-done((bf16[256,2048]{1,0:T(8,128)(2,1)}, bf16[256,2048]{1,0:T(8,128)(2,1)}, u32[]{:S(2)}, u32[]{:S(2)}) %collective-permute-start) | collective-permute-done | bytes 1048608 | tf_op jit(solution)/shard_map/ppermute | solution.py:156
  113.7 1.7 collective-permute-done.1
  115.4 1.6 collective-permute-start.5
  117.1 1.3 collective-permute-start.6
  118.4 47.3 %attention_level.4 = (bf16[4,1,256,2048]{3,2,1,0:T(8,128)(2,1)}, f32[4,256,256]{2,1,0:T(8,128)S(1)}, f32[4,256,256]{2,1,0:T(8,128)S(1)}) custom-call(s32[8]{0:T(128)S(1)} %stack.48.info_ref, bf16[4,1,256,2048]{3,2,1,0:T(8,128)(2,1)} %q_ref.7, bf16[256,8192]{1,0:T(8,128)(2,1)} %bitcast.49, bf16[2048,8192]{1,0:T(8,128)(2,1)} %weight_ref.7, ...), custom_call_target="tpu_custom_call" | custom-call | flops 30064771072 | bytes 36700160 | tf_op jit(solution)/shard_map/attention_level/pallas_call | solution.py:112
  168.1 1.2 select_convert_fusion
  169.4 1.3 stack.106.info_ref
  170.7 2.0 stack.103.info_ref
  172.6 2.4 broadcast_in_dim.172
  175.1 2.4 constant_dynamic-update-slice_fusion
  178.3 0.9 pad_maximum_fusion.3
  179.2 32.6 %all-gather.11.cloned.1.call-done = bf16[1,1,256,8192]{3,2,1,0:T(8,128)(2,1)} async-done(((bf16[1,1,256,2048]{3,2,1,0:T(8,128)(2,1)}), bf16[1,1,256,8192]{3,2,1,0:T(8,128)(2,1)}) %all-gather.11.cloned.1.call-update) | async-done | bytes 4194320 | tf_op jit(solution)/shard_map/all_gather | solution.py:147
  211.7 1.7 convert_add_fusion.2
  213.5 1.5 collective-permute-start.10
  215.0 0.9 collective-permute-start.7
  215.9 42.0 %attention_level.5 = (bf16[4,1,256,2048]{3,2,1,0:T(8,128)(2,1)}, f32[3,256,256]{2,1,0:T(8,128)S(1)}, f32[3,256,256]{2,1,0:T(8,128)S(1)}) custom-call(s32[8]{0:T(128)S(1)} %stack.103.info_ref, bf16[4,1,256,2048]{3,2,1,0:T(8,128)(2,1)} %q_ref.7, bf16[256,8192]{1,0:T(8,128)(2,1)} %bitcast.47, ...), custom_call_target="tpu_custom_call", output_to_operand_aliasing={{0}: (10, {})} | custom-call | flops 24696061952 | bytes 36700160 | tf_op jit(solution)/shard_map/attention_level/pallas_call | solution.py:112
  258.3 1.4 collective-permute-start.11
  259.8 1.4 add_convert_fusion
  261.1 1.3 collective-permute-start.8
  262.5 3.4 collective-permute-done.11
  266.0 2.6 select_dynamic-update-slice_fusion.2
  268.6 2.6 select_dynamic-update-slice_fusion.1
  271.2 41.4 %collective-permute-done.8 = bf16[256,2048]{1,0:T(8,128)(2,1)S(1)} collective-permute-done((bf16[256,2048]{1,0:T(8,128)(2,1)}, bf16[256,2048]{1,0:T(8,128)(2,1)S(1)}, u32[]{:S(2)}, u32[]{:S(2)}) %collective-permute-start.8) | collective-permute-done | bytes 1048608 | tf_op jit(solution)/shard_map/ppermute | solution.py:157
  312.6 1.4 select_dynamic-update-slice_fusion.cot_ref
  314.0 33.7 %attention_level.6 = (bf16[4,1,256,2048]{3,2,1,0:T(8,128)(2,1)}, f32[2,256,256]{2,1,0:T(8,128)S(1)}, f32[2,256,256]{2,1,0:T(8,128)S(1)}) custom-call(s32[8]{0:T(128)S(1)} %stack.106.info_ref, bf16[4,1,256,2048]{3,2,1,0:T(8,128)(2,1)} %q_ref.7, bf16[256,8192]{1,0:T(8,128)(2,1)} %select_dynamic-update-slice_fusion.cot_ref, ...), custom_call_target="tpu_custom_call", output_to_operand_aliasing={{0}: (8, {})} | custom-call | flops 19327352832 | bytes 36700160 | tf_op jit(solution)/shard_map/attention_level/pallas_call | solution.py:112
  349.2 1.4 add_convert_fusion.1
  351.6 2.1 fusion.15
  353.7 1.5 collective-permute-start.16
  355.3 1.8 fusion.16
  357.8 10.7 %collective-permute-done.16 = bf16[2,2,256,256]{3,2,1,0:T(8,128)(2,1)S(1)} collective-permute-done((bf16[2,2,256,256]{3,2,1,0:T(8,128)(2,1)S(1)}, bf16[2,2,256,256]{3,2,1,0:T(8,128)(2,1)S(1)}, u32[]{:S(2)}, u32[]{:S(2)}) %collective-permute-start.16) | collective-permute-done | bytes 524320 | tf_op jit(solution)/shard_map/ppermute | solution.py:139
  368.7 1.6 collective-permute-start.17
  370.3 9.0 %collective-permute-done.13 = bf16[2,2,256,256]{3,2,1,0:T(8,128)(2,1)S(1)} collective-permute-done((bf16[2,2,256,256]{3,2,1,0:T(8,128)(2,1)S(1)}, bf16[2,2,256,256]{3,2,1,0:T(8,128)(2,1)S(1)}, u32[]{:S(2)}, u32[]{:S(2)}) %collective-permute-start.13) | collective-permute-done | bytes 524320 | tf_op jit(solution)/shard_map/ppermute | solution.py:139
  379.4 1.5 collective-permute-start.14
  381.1 6.3 %collective-permute-done.14 = bf16[1,2,256,256]{3,2,1,0:T(8,128)(2,1)S(1)} collective-permute-done((bf16[1,2,256,256]{3,2,1,0:T(8,128)(2,1)S(1)}, bf16[1,2,256,256]{3,2,1,0:T(8,128)(2,1)S(1)}, u32[]{:S(2)}, u32[]{:S(2)}) %collective-permute-start.14) | collective-permute-done | bytes 262176 | tf_op jit(solution)/shard_map/ppermute | solution.py:139
  387.5 2.2 copy-done.2
  389.6 26.3 %attention_level.7 = (bf16[4,1,256,2048]{3,2,1,0:T(8,128)(2,1)}, f32[1,256,256]{2,1,0:T(8,128)S(1)}, f32[1,256,256]{2,1,0:T(8,128)S(1)}) custom-call(s32[8]{0:T(128)S(1)} %stack.44.info_ref, bf16[4,1,256,2048]{3,2,1,0:T(8,128)(2,1)S(1)} %copy-done.2, bf16[256,8192]{1,0:T(8,128)(2,1)} %bitcast.48, ...), custom_call_target="tpu_custom_call", output_to_operand_aliasing={{0}: (6, {})} | custom-call | flops 13958643712 | bytes 36700160 | tf_op jit(solution)/shard_map/attention_level/pallas_call | solution.py:112
  416.1 0.9 maximum_bitcast_fusion.2
  (112 shorter events, 12.1 us)
Async XLA Ops:
  7.2 108.3 %all-gather.9.cloned.1.call-start = ((), (), s32[]{:S(2)}) async-start(), calls=%async_computation.1 | async-start | bytes 5242880 | tf_op jit(solution)/shard_map/all_gather | solution.py:147
  11.6 1.0 slice-start
  11.6 1.1 slice-start.1
  11.6 200.1 %all-gather.11.cloned.1.call-start = ((), (), s32[]{:S(2)}) async-start(), calls=%async_computation.2 | async-start | bytes 5242880 | tf_op jit(solution)/shard_map/all_gather | solution.py:147
  12.8 20.6 %collective-permute-start.2 = (bf16[1,3,2,256,256]{4,3,2,1,0:T(8,128)(2,1)S(1)}, bf16[1,3,2,256,256]{4,3,2,1,0:T(8,128)(2,1)S(1)}, u32[]{:S(2)}, u32[]{:S(2)}) collective-permute-start(bf16[1,3,2,256,256]{4,3,2,1,0:T(8,128)(2,1)S(1)} %maximum_bitcast_fusion), channel_id=1, source_target_pairs={{0,16},{4,20},{8,24},{12,28},{16,0},{20,4},{24,8},{28,12},{1,17},{... | collective-permute-start | bytes 2359304 | tf_op jit(solution)/shard_map/ppermute | solution.py:139
  33.5 43.7 %copy-start.19 = (s32[3,8]{1,0:T(4,128)S(1)}, s32[3,8]{1,0:T(4,128)}, u32[]{:S(2)}) copy-start(s32[3,8]{1,0:T(4,128)} %param.24) | copy-start | bytes 292
  33.5 61.0 %copy-start.18 = (s32[4,8]{1,0:T(4,128)S(1)}, s32[4,8]{1,0:T(4,128)}, u32[]{:S(2)}) copy-start(s32[4,8]{1,0:T(4,128)} %param.25) | copy-start | bytes 388
  33.5 65.0 %copy-start.20 = (s32[4]{0:T(128)S(1)}, s32[4]{0:T(128)}, u32[]{:S(2)}) copy-start(s32[4]{0:T(128)} %constant.105.clone) | copy-start | bytes 52
  33.5 35.8 %collective-permute-start.3 = (bf16[2,3,2,256,256]{4,3,2,1,0:T(8,128)(2,1)S(1)}, bf16[2,3,2,256,256]{4,3,2,1,0:T(8,128)(2,1)S(1)}, u32[]{:S(2)}, u32[]{:S(2)}) collective-permute-start(bf16[2,3,2,256,256]{4,3,2,1,0:T(8,128)(2,1)S(1)} %pad_maximum_fusion.2), channel_id=1, source_target_pairs={{0,8},{4,12},{8,0},{12,4},{16,24},{20,28},{24,16},{28,20},{1,9},{5... | collective-permute-start | bytes 4718600 | tf_op jit(solution)/shard_map/ppermute | solution.py:139
  69.3 2.2 copy-start.3
  71.5 27.1 %collective-permute-start.4 = (bf16[4,3,2,256,256]{4,3,2,1,0:T(8,128)(2,1)}, bf16[4,3,2,256,256]{4,3,2,1,0:T(8,128)(2,1)}, u32[]{:S(2)}, u32[]{:S(2)}) collective-permute-start(bf16[4,3,2,256,256]{4,3,2,1,0:T(8,128)(2,1)} %pad_maximum_fusion.1), channel_id=1, source_target_pairs={{0,4},{4,0},{8,12},{12,8},{16,20},{20,16},{24,28},{28,24},{1,5},{5... | collective-permute-start | bytes 9437192 | tf_op jit(solution)/shard_map/ppermute | solution.py:139
  71.5 316.0 %all-gather.7.cloned.1.call-start = ((), (), s32[]{:S(2)}) async-start(), calls=%async_computation | async-start | bytes 5242880 | tf_op jit(solution)/shard_map/all_gather | solution.py:147
  71.5 42.1 %collective-permute-start = (bf16[256,2048]{1,0:T(8,128)(2,1)}, bf16[256,2048]{1,0:T(8,128)(2,1)}, u32[]{:S(2)}, u32[]{:S(2)}) collective-permute-start(bf16[256,2048]{1,0:T(8,128)(2,1)} %get-tuple-element.61), channel_id=1, source_target_pairs={{0,1},{1,2},{2,3},{4,5},{5,6},{6,7},{8,9},{9,10},{10,11},{12,13},{... | collective-permute-start | bytes 3145736 | tf_op jit(solution)/shard_map/ppermute | solution.py:156
  75.9 39.5 %collective-permute-start.1 = (bf16[256,2048]{1,0:T(8,128)(2,1)}, bf16[256,2048]{1,0:T(8,128)(2,1)}, u32[]{:S(2)}, u32[]{:S(2)}) collective-permute-start(bf16[256,2048]{1,0:T(8,128)(2,1)} %get-tuple-element.61), channel_id=1, source_target_pairs={{1,0},{2,1},{3,2},{5,4},{6,5},{7,6},{9,8},{10,9},{11,10},{13,12},{... | collective-permute-start | bytes 3145736 | tf_op jit(solution)/shard_map/ppermute | solution.py:157
  98.5 19.9 %copy-start = (bf16[4,1,256,256]{3,2,1,0:T(8,128)(2,1)S(1)}, bf16[4,1,256,256]{3,2,1,0:T(8,128)(2,1)}, u32[]{:S(2)}) copy-start(bf16[4,1,256,256]{3,2,1,0:T(8,128)(2,1)} %refs_0_.1) | copy-start | bytes 1572868
  98.5 19.9 %copy-start.1 = (bf16[4,1,256,256]{3,2,1,0:T(8,128)(2,1)S(1)}, bf16[4,1,256,256]{3,2,1,0:T(8,128)(2,1)}, u32[]{:S(2)}) copy-start(bf16[4,1,256,256]{3,2,1,0:T(8,128)(2,1)} %refs_1_.3) | copy-start | bytes 1572868
  115.4 96.3 %collective-permute-start.5 = (bf16[256,2048]{1,0:T(8,128)(2,1)}, bf16[256,2048]{1,0:T(8,128)(2,1)}, u32[]{:S(2)}, u32[]{:S(2)}) collective-permute-start(bf16[256,2048]{1,0:T(8,128)(2,1)} %collective-permute-done), channel_id=1, source_target_pairs={{1,2},{2,3},{5,6},{6,7},{9,10},{10,11},{13,14},{14,15},{17,18},{18... | collective-permute-start | bytes 3145736 | tf_op jit(solution)/shard_map/ppermute | solution.py:156
  117.1 94.7 %collective-permute-start.6 = (bf16[256,2048]{1,0:T(8,128)(2,1)}, bf16[256,2048]{1,0:T(8,128)(2,1)}, u32[]{:S(2)}, u32[]{:S(2)}) collective-permute-start(bf16[256,2048]{1,0:T(8,128)(2,1)} %collective-permute-done.1), channel_id=1, source_target_pairs={{1,0},{2,1},{5,4},{6,5},{9,8},{10,9},{13,12},{14,13},{17,16},{18,1... | collective-permute-start | bytes 3145736 | tf_op jit(solution)/shard_map/ppermute | solution.py:157
  167.3 0.8 copy-start.4
  169.3 42.4 %collective-permute-start.9 = (bf16[4,2,256,256]{3,2,1,0:T(8,128)(2,1)}, bf16[4,2,256,256]{3,2,1,0:T(8,128)(2,1)}, u32[]{:S(2)}, u32[]{:S(2)}) collective-permute-start(bf16[4,2,256,256]{3,2,1,0:T(8,128)(2,1)} %select_convert_fusion), channel_id=1, source_target_pairs={{0,4},{4,0},{8,12},{12,8},{16,20},{20,16},{24,28},{28,24},{1,5},{5... | collective-permute-start | bytes 3145736 | tf_op jit(solution)/shard_map/ppermute | solution.py:139
  175.1 2.4 copy-start.13
  175.1 2.4 copy-start.15
  175.1 3.2 copy-start.14
  213.5 44.7 %collective-permute-start.10 = (bf16[2,2,256,256]{3,2,1,0:T(8,128)(2,1)S(1)}, bf16[2,2,256,256]{3,2,1,0:T(8,128)(2,1)S(1)}, u32[]{:S(2)}, u32[]{:S(2)}) collective-permute-start(bf16[2,2,256,256]{3,2,1,0:T(8,128)(2,1)S(1)} %slice.196), channel_id=1, source_target_pairs={{0,8},{4,12},{8,0},{12,4},{16,24},{20,28},{24,16},{28,20},{1,9},{5... | collective-permute-start | bytes 1572872 | tf_op jit(solution)/shard_map/ppermute | solution.py:139
  215.0 51.0 %collective-permute-start.7 = (bf16[256,2048]{1,0:T(8,128)(2,1)}, bf16[256,2048]{1,0:T(8,128)(2,1)S(1)}, u32[]{:S(2)}, u32[]{:S(2)}) collective-permute-start(bf16[256,2048]{1,0:T(8,128)(2,1)} %collective-permute-done.5), channel_id=1, source_target_pairs={{2,3},{6,7},{10,11},{14,15},{18,19},{22,23},{26,27},{30,31}} | collective-permute-start | bytes 3145736 | tf_op jit(solution)/shard_map/ppermute | solution.py:156
  258.1 1.7 copy-start.11
  258.1 3.0 copy-start.12
  258.3 7.6 %collective-permute-start.11 = (bf16[1,2,256,256]{3,2,1,0:T(8,128)(2,1)S(1)}, bf16[1,2,256,256]{3,2,1,0:T(8,128)(2,1)S(1)}, u32[]{:S(2)}, u32[]{:S(2)}) collective-permute-start(bf16[1,2,256,256]{3,2,1,0:T(8,128)(2,1)S(1)} %slice.261), channel_id=1, source_target_pairs={{0,16},{4,20},{8,24},{12,28},{16,0},{20,4},{24,8},{28,12},{1,17},{... | collective-permute-start | bytes 786440 | tf_op jit(solution)/shard_map/ppermute | solution.py:139
  261.1 90.4 %collective-permute-start.15 = (bf16[4,2,256,256]{3,2,1,0:T(8,128)(2,1)}, bf16[4,2,256,256]{3,2,1,0:T(8,128)(2,1)}, u32[]{:S(2)}, u32[]{:S(2)}) collective-permute-start(bf16[4,2,256,256]{3,2,1,0:T(8,128)(2,1)} %add_convert_fusion), channel_id=1, source_target_pairs={{0,4},{4,0},{8,12},{12,8},{16,20},{20,16},{24,28},{28,24},{1,5},{5... | collective-permute-start | bytes 3145736 | tf_op jit(solution)/shard_map/ppermute | solution.py:139
  261.1 51.5 %collective-permute-start.8 = (bf16[256,2048]{1,0:T(8,128)(2,1)}, bf16[256,2048]{1,0:T(8,128)(2,1)S(1)}, u32[]{:S(2)}, u32[]{:S(2)}) collective-permute-start(bf16[256,2048]{1,0:T(8,128)(2,1)} %collective-permute-done.6), channel_id=1, source_target_pairs={{1,0},{5,4},{9,8},{13,12},{17,16},{21,20},{25,24},{29,28}} | collective-permute-start | bytes 3145736 | tf_op jit(solution)/shard_map/ppermute | solution.py:157
  262.5 86.8 %copy-start.7 = (f32[2,256,256]{2,1,0:T(8,128)}, f32[2,256,256]{2,1,0:T(8,128)S(1)}, u32[]{:S(2)}) copy-start(f32[2,256,256]{2,1,0:T(8,128)S(1)} %pad_maximum_fusion.4) | copy-start | bytes 1572868
  347.7 1.5 copy-start.5
  349.2 1.6 copy-start.9
  350.7 4.6 %collective-permute-start.12 = (bf16[4,2,256,256]{3,2,1,0:T(8,128)(2,1)}, bf16[4,2,256,256]{3,2,1,0:T(8,128)(2,1)}, u32[]{:S(2)}, u32[]{:S(2)}) collective-permute-start(bf16[4,2,256,256]{3,2,1,0:T(8,128)(2,1)} %add_convert_fusion.1), channel_id=1, source_target_pairs={{0,4},{4,0},{8,12},{12,8},{16,20},{20,16},{24,28},{28,24},{1,5},{5... | collective-permute-start | bytes 3145736 | tf_op jit(solution)/shard_map/ppermute | solution.py:139
  351.6 3.7 copy-start.6
  351.6 3.7 copy-start.8
  351.6 3.7 copy-start.10
  353.7 14.8 %collective-permute-start.16 = (bf16[2,2,256,256]{3,2,1,0:T(8,128)(2,1)S(1)}, bf16[2,2,256,256]{3,2,1,0:T(8,128)(2,1)S(1)}, u32[]{:S(2)}, u32[]{:S(2)}) collective-permute-start(bf16[2,2,256,256]{3,2,1,0:T(8,128)(2,1)S(1)} %slice.210), channel_id=1, source_target_pairs={{0,8},{4,12},{8,0},{12,4},{16,24},{20,28},{24,16},{28,20},{1,9},{5... | collective-permute-start | bytes 1572872 | tf_op jit(solution)/shard_map/ppermute | solution.py:139
  357.2 22.1 %collective-permute-start.13 = (bf16[2,2,256,256]{3,2,1,0:T(8,128)(2,1)S(1)}, bf16[2,2,256,256]{3,2,1,0:T(8,128)(2,1)S(1)}, u32[]{:S(2)}, u32[]{:S(2)}) collective-permute-start(bf16[2,2,256,256]{3,2,1,0:T(8,128)(2,1)S(1)} %slice.202), channel_id=1, source_target_pairs={{0,8},{4,12},{8,0},{12,4},{16,24},{20,28},{24,16},{28,20},{1,9},{5... | collective-permute-start | bytes 1572872 | tf_op jit(solution)/shard_map/ppermute | solution.py:139
  368.6 12.3 %copy-start.16 = (f32[1,256,256]{2,1,0:T(8,128)S(1)}, f32[1,256,256]{2,1,0:T(8,128)}, u32[]{:S(2)}) copy-start(f32[1,256,256]{2,1,0:T(8,128)} %get-tuple-element.76) | copy-start | bytes 786436
  368.7 12.3 %copy-start.17 = (f32[1,256,256]{2,1,0:T(8,128)S(1)}, f32[1,256,256]{2,1,0:T(8,128)}, u32[]{:S(2)}) copy-start(f32[1,256,256]{2,1,0:T(8,128)} %get-tuple-element.78) | copy-start | bytes 786436
  368.7 12.3 %collective-permute-start.17 = (bf16[1,2,256,256]{3,2,1,0:T(8,128)(2,1)S(1)}, bf16[1,2,256,256]{3,2,1,0:T(8,128)(2,1)S(1)}, u32[]{:S(2)}, u32[]{:S(2)}) collective-permute-start(bf16[1,2,256,256]{3,2,1,0:T(8,128)(2,1)S(1)} %slice.259), channel_id=1, source_target_pairs={{0,16},{4,20},{8,24},{12,28},{16,0},{20,4},{24,8},{28,12},{1,17},{... | collective-permute-start | bytes 786440 | tf_op jit(solution)/shard_map/ppermute | solution.py:139
  379.4 7.9 %collective-permute-start.14 = (bf16[1,2,256,256]{3,2,1,0:T(8,128)(2,1)S(1)}, bf16[1,2,256,256]{3,2,1,0:T(8,128)(2,1)S(1)}, u32[]{:S(2)}, u32[]{:S(2)}) collective-permute-start(bf16[1,2,256,256]{3,2,1,0:T(8,128)(2,1)S(1)} %slice.260), channel_id=1, source_target_pairs={{0,16},{4,20},{8,24},{12,28},{16,0},{20,4},{24,8},{28,12},{1,17},{... | collective-permute-start | bytes 786440 | tf_op jit(solution)/shard_map/ppermute | solution.py:139
  387.5 2.2 copy-start.2
Sparse Core Ops, SparseCore 0:
  11.7 94.7 all-gather.8
  108.1 103.5 all-gather.10
  213.3 89.5 all-gather.6

commit v3 on v2

--- a/solution.py
+++ b/solution.py
@@ -18,12 +18,14 @@
     return lax.dynamic_index_in_dim(table, index_value, 0, keepdims=False)
 
 
-def attention_kernel(level, has_base, info_ref, q_ref, cot_ref, weight_ref, *refs):
+def attention_kernel(level, fused, has_base, info_ref, q_ref, cot_ref, *refs):
     blocks = level + 1
+    if fused:
+        weight_ref, refs = refs[0], refs[1:]
     key_refs, value_refs = refs[:blocks], refs[blocks : 2 * blocks]
     dq_ref, dk_ref, dv_ref = refs[2 * blocks + has_base :]
     seg = cot_ref.shape[0]
-    heads = weight_ref.shape[0] // HD
+    heads = q_ref.shape[3] // HD
     scale = 1.0 / HD**0.5
     own_len = info_ref[4 + level]
     keys = [ref[...].reshape(seg, HD) for ref in key_refs]
@@ -39,7 +41,10 @@
         dk_ref[...] = jnp.zeros_like(dk_ref)
         dv_ref[...] = jnp.zeros_like(dv_ref)
 
-    douts = dot(cot_ref[...], weight_ref[...], NT).astype(jnp.bfloat16)
+    if fused:
+        douts = dot(cot_ref[...], weight_ref[...], NT).astype(jnp.bfloat16)
+    else:
+        douts = cot_ref[...]
     row = lax.broadcasted_iota(jnp.int32, douts.shape, 0)
     douts = jnp.where(row < own_len, douts, jnp.zeros_like(douts))
     for h in range(heads):
@@ -51,9 +56,9 @@
             allowed = key_pos < info_ref[4 + m]
             if m == level:
                 allowed = allowed & (key_pos <= query_pos)
-            scores.append(jnp.where(allowed, dot(keys[m], q, NT) * scale, MASKED))
+            scores.append(jnp.where(allowed, dot(keys[m], q, NT), MASKED))
         top = functools.reduce(jnp.maximum, [jnp.max(s, axis=0, keepdims=True) for s in scores])
-        exps = [jnp.exp(s - top) for s in scores]
+        exps = [jnp.exp((s - top) * scale) for s in scores]
         total = functools.reduce(jnp.add, [jnp.sum(e, axis=0, keepdims=True) for e in exps])
         inverse = 1.0 / total
         probs = [e * inverse for e in exps]
@@ -75,15 +80,15 @@
         dq_ref[0, 0, :, columns] = (dq * scale).T.astype(jnp.bfloat16)
 
 
-def attention_level(level, info, queries, cot, weight, key_rows, value_rows, kv_all, base):
+def attention_level(level, row_block, info, queries, cot, weight, key_rows, value_rows, kv_all, base):
     levels, _, seg, q_width = queries.shape
     kv_width = key_rows.shape[3]
     kv_local = kv_width // HD
     group = q_width // kv_width
     blocks = level + 1
-    heads = 2
+    heads = min(4, group)
     steps = group // heads
-    model = weight.shape[1]
+    fused = weight is not None
 
     def gathered(kind, m):
         return pl.BlockSpec(
@@ -94,13 +99,25 @@
         (1, 1, seg, heads * HD), lambda n, g, info: (level, 0, 0, n * steps + g)
     )
     own_spec = pl.BlockSpec((1, 1, seg, HD), lambda n, g, info: (level, 0, 0, n))
-    cot_spec = pl.BlockSpec((seg, model), lambda n, g, info: (0, 0))
-    weight_spec = pl.BlockSpec((heads * HD, model), lambda n, g, info: (n * steps + g, 0))
+    if fused:
+        model = weight.shape[1]
+        products_in = 2 * seg * model * q_width
+        cot_specs = [
+            pl.BlockSpec((seg, model), lambda n, g, info: (row_block, 0)),
+            pl.BlockSpec((heads * HD, model), lambda n, g, info: (n * steps + g, 0)),
+        ]
+        cots = [cot, weight]
+    else:
+        products_in = 0
+        cot_specs = [
+            pl.BlockSpec((seg, heads * HD), lambda n, g, info: (row_block, n * steps + g))
+        ]
+        cots = [cot]
     grad_spec = pl.BlockSpec((blocks, seg, HD), lambda n, g, info: (0, 0, n))
-    in_specs = [q_spec, cot_spec, weight_spec]
+    in_specs = [q_spec] + cot_specs
     in_specs += [gathered(0, m) for m in range(level)] + [own_spec]
     in_specs += [gathered(1, m) for m in range(level)] + [own_spec]
-    operands = [queries, cot, weight]
+    operands = [queries] + cots
     operands += [kv_all] * level + [key_rows] + [kv_all] * level + [value_rows]
     aliases = {}
     if base is not None:
@@ -110,7 +127,7 @@
     grad_shape = jax.ShapeDtypeStruct((blocks, seg, kv_width), jnp.float32)
     products = 5 * 2 * seg * seg * HD * blocks * kv_local * group
     return pl.pallas_call(
-        functools.partial(attention_kernel, level, int(base is not None)),
+        functools.partial(attention_kernel, level, fused, int(base is not None)),
         grid_spec=pltpu.PrefetchScalarGridSpec(
             num_scalar_prefetch=1,
             grid=(kv_local, steps),
@@ -119,17 +136,17 @@
         ),
         out_shape=[jax.ShapeDtypeStruct(queries.shape, jnp.bfloat16), grad_shape, grad_shape],
         input_output_aliases=aliases,
-        compiler_params=pltpu.CompilerParams(vmem_limit_bytes=48 * 1024 * 1024),
+        compiler_params=pltpu.CompilerParams(vmem_limit_bytes=52 * 1024 * 1024),
         cost_estimate=pl.CostEstimate(
-            flops=4 * products + 2 * seg * model * q_width,
-            bytes_accessed=3 * seg * q_width * 2 + q_width * model * 2,
+            flops=4 * products + products_in,
+            bytes_accessed=3 * seg * q_width * 2,
             transcendentals=seg * seg * blocks * kv_local * group,
         ),
         name="attention_level",
     )(info, *operands)
 
 
-def local(node_count, head_count, queries, key_rows, value_rows, cotangent, out_weight, parents, seg_len):
+def local(node_count, queries, key_rows, value_rows, cotangent, out_weight, parents, seg_len):
     levels, _, seg, q_width = queries.shape
     bits = node_count.bit_length() - 1
     me = lax.axis_index("branch")
@@ -138,27 +155,23 @@
         pairs = [(i, i ^ (1 << bit)) for i in range(node_count)]
         return lax.ppermute(array, "branch", pairs)
 
-    line_level = 1
-    place = lax.axis_index("head")
     width = cotangent.shape[3]
-    gathered = [None] * levels
-    for level in reversed(range(levels)):
-        if level != line_level:
-            gathered[level] = lax.all_gather(cotangent[level, 0], "head", axis=1, tiled=True)
-    line = cotangent[line_level, 0]
-    uphill = [line]
-    downhill = [line]
-
-    def hop():
-        done = len(uphill)
-        up = [(i, i + 1) for i in range(done - 1, head_count - 1)]
-        down = [(i + 1, i) for i in range(head_count - done)]
-        uphill.append(lax.ppermute(uphill[-1], "head", up))
-        downhill.append(lax.ppermute(downhill[-1], "head", down))
-
+    gathered = {}
+
+    def gather(first, last, rows):
+        rows = rows.reshape((last - first) * seg, width)
+        gathered[first] = lax.all_gather(rows, "head", axis=1, tiled=True)
+
+    gather(levels - 2, levels, cotangent[levels - 2 :, 0])
     kv_all = jnp.stack([key_rows[: levels - 1, 0], value_rows[: levels - 1, 0]], axis=1)[None]
+    waiting = list(range(levels - 2))
     for bit in reversed(range(bits)):
-        kv_all = jnp.concatenate([kv_all, swap(kv_all, bit)], axis=0)
+        arrived = swap(kv_all, bit)
+        if bit < len(waiting):
+            level = waiting.pop()
+            rows, arrived = lax.optimization_barrier((cotangent[level, 0], arrived))
+            gather(level, level + 1, rows)
+        kv_all = jnp.concatenate([kv_all, arrived], axis=0)
 
     offsets = []
     infos = []
@@ -177,35 +190,24 @@
         offsets.append(relative)
 
     key_terms = [[] for _ in range(levels)]
-    received = [None] * levels
+    received = [None] * (levels - 1)
     key_grads = [None] * levels
     value_grads = [None] * levels
     query_grad = None
     for level in reversed(range(levels)):
-        if level == line_level:
-            while len(uphill) < head_count:
-                hop()
-            whole = jnp.zeros((seg, head_count * width), cotangent.dtype)
-            whole = lax.dynamic_update_slice(whole, line, (0, place * width))
-            for j in range(1, head_count):
-                ahead = place + j < head_count
-                piece = jnp.where(ahead, downhill[j], uphill[head_count - j])
-                at = lax.rem(place + j, head_count) * width
-                whole = lax.dynamic_update_slice(whole, piece, (0, at))
-            gathered[level] = whole
-        elif level > line_level and len(uphill) < head_count:
-            hop()
-            gathered[level], uphill[-1], downhill[-1] = lax.optimization_barrier(
-                (gathered[level], uphill[-1], downhill[-1])
-            )
-        if level <= line_level:
-            due = range(level + 1 if level else 0, levels - 1)
-            for m in due:
-                gathered[level], received[m] = lax.optimization_barrier(
-                    (gathered[level], received[m])
-                )
+        first = min(level, levels - 2)
+        if level == 0:
+            gathered[0], *received = lax.optimization_barrier((gathered[0], *received))
+        if level == 0:
+            cot, weight = gathered[0], out_weight
+        else:
+            if level == levels - 1 or level < levels - 2:
+                dout = lax.dot_general(
+                    gathered[first], out_weight, NT, preferred_element_type=jnp.float32
+                ).astype(jnp.bfloat16)
+            cot, weight = dout, None
         query_grad, dk, dv = attention_level(
-            level, infos[level], queries, gathered[level], out_weight,
+            level, level - first, infos[level], queries, cot, weight,
             key_rows, value_rows, kv_all, query_grad,
         )
         own = jnp.stack([dk[level], dv[level]])
@@ -242,7 +244,7 @@
     wide = P(None, "branch", None, "head")
     in_specs = (wide, wide, wide, wide, P("head", None), P(), P())
     return jax.shard_map(
-        functools.partial(local, mesh.shape["branch"], mesh.shape["head"]),
+        functools.partial(local, mesh.shape["branch"]),
         mesh=mesh,
         in_specs=in_specs,
         out_specs=(wide, wide, wide),

time: 425 us -> 460 us (1.082)
  waiting for transfers between devices: 166 us -> 263 us
  Pallas kernels: 149 us -> 76.6 us
  matrix products: 0 us -> 43 us
  other arithmetic: 28.6 us -> 12.4 us
  starting transfers between devices: 24 us -> 13.9 us
  local copies, waits for them, and re-layouts: 26.5 us -> 20.3 us
    all_gather x3, waiting for transfers between devices: 32.6 us -> 178 us  [gather(): gathered[first] = lax.all_gather(rows, 'head', axis=1, tiled=True)]
    pallas_call x4, Pallas kernels: 149 us -> 76.6 us  [attention_level(): pl.pallas_call(functools.partial(attention_kernel, level, fused, int(base...]
    ppermute x6 -> x0, waiting for transfers between devices: 52.5 us -> none  [the longest x3 43.2 us: hop(): downhill.append(lax.ppermute(downhill[-1], 'head', down))]
    dot_general x0 -> x2, matrix products: none -> 43 us  [local(): lax.dot_general(gathered[first], out_weight, NT, preferred_element_type=j...]
    ppermute x6 -> x0, starting transfers between devices: 10.8 us -> none  [the longest x3 6.94 us: hop(): uphill.append(lax.ppermute(uphill[-1], 'head', up))]
    dynamic_update_slice x3 -> x0, other arithmetic: 6.58 us -> none  [local(): whole = lax.dynamic_update_slice(whole, piece, (0, at))]
  transfers between devices with their start and end apart: 21 -> 15, of which waited for: 10 -> 8; matrix products, arithmetic and copies ran while one was open for 11% -> 15% of each run, Pallas kernels for 29% -> 12%
where the time goes in v3:
time: 460 us; the launch traced here: 459 us
  waiting for transfers between devices  263 us (57%)
  Pallas kernels  76.6 us (17%)
  matrix products  43 us (9%)
  between operations  29.4 us (6%)
  local copies, waits for them, and re-layouts  20.3 us (4%)
  starting transfers between devices  13.9 us (3%)
  other arithmetic  12.4 us (3%)
    all_gather x3, waiting for transfers between devices, gather(): gathered[first] = lax.all_gather(rows, 'head', axis=1, tiled=True)  178 us
    ppermute x12, waiting for transfers between devices, swap(): return lax.ppermute(array, 'branch', pairs)  84.8 us
    pallas_call x4, Pallas kernels, attention_level(): pl.pallas_call(functools.partial(attention_kernel, level, fused, int(base...  76.6 us
    dot_general x2, matrix products, local(): lax.dot_general(gathered[first], out_weight, NT, preferred_element_type=j...  43 us
    ppermute x12, starting transfers between devices, swap(): return lax.ppermute(array, 'branch', pairs)  13.8 us
  transfers between devices with their start and end apart: 15, of which 8 were waited for; matrix products, arithmetic and copies ran while one was open for 15% of the time, Pallas kernels for 12%

profile of v3, /device:TPU:0, one launch (start us, length us, event | category | flops | bytes accessed | tf_op | source)
XLA Modules:
  0.0 458.8 jit_solution(3784241572808064188)
XLA Ops:
  7.2 1.0 slice.175
  8.2 1.0 slice.176
  9.4 3.0 collective-permute-start
  12.4 17.5 %collective-permute-done = bf16[1,3,2,256,256]{4,3,2,1,0:T(8,128)(2,1)S(1)} collective-permute-done((bf16[1,3,2,256,256]{4,3,2,1,0:T(8,128)(2,1)S(1)}, bf16[1,3,2,256,256]{4,3,2,1,0:T(8,128)(2,1)S(1)}, u32[]{:S(2)}, u32[]{:S(2)}) %collective-permute-start) | collective-permute-done | bytes 786464 | tf_op jit(solution)/shard_map/ppermute | solution.py:156
  30.1 1.8 collective-permute-start.1
  31.9 1.5 slice_bitcast_fusion
  33.4 32.4 %collective-permute-done.1 = bf16[2,3,2,256,256]{4,3,2,1,0:T(8,128)(2,1)S(1)} collective-permute-done((bf16[2,3,2,256,256]{4,3,2,1,0:T(8,128)(2,1)S(1)}, bf16[2,3,2,256,256]{4,3,2,1,0:T(8,128)(2,1)S(1)}, u32[]{:S(2)}, u32[]{:S(2)}) %collective-permute-start.1) | collective-permute-done | bytes 1572896 | tf_op jit(solution)/shard_map/ppermute | solution.py:156
  65.8 3.1 slice.184
  69.0 2.0 pad_maximum_fusion.1
  71.0 0.6 constant_dynamic-slice_fusion.14
  73.6 0.6 constant_dynamic-slice_fusion.13
  78.6 0.7 constant_dynamic-slice_fusion.12
  88.2 0.7 constant_dynamic-slice_fusion.10
  88.9 0.6 stack.44.info_ref
  89.6 1.3 stack.106.info_ref
  90.8 0.6 constant_dynamic-slice_fusion.9
  91.4 1.9 stack.103.info_ref
  93.4 2.6 stack.49.info_ref
  96.0 5.1 %pad_maximum_fusion.refs_0_.refs_1_.refs_2_.refs_4_.refs_5_.refs_6_.refs_3_ = bf16[8,3,2,256,256]{4,3,2,1,0:T(8,128)(2,1)} fusion(bf16[4,3,2,256,256]{4,3,2,1,0:T(8,128)(2,1)} %collective-permute-done.2, bf16[2,3,2,256,256]{4,3,2,1,0:T(8,128)(2,1)S(1)} %collective-permute-done.1, bf16[1,3,2,256,256]{4,3,2,1,0:T(8,128)(2,1)S(1)} %collective-permute-done, ...), kind=kLoop, calls=%fused_computation | loop fusion | flops 9437184 | bytes 12582912 | tf_op jit(solution)/shard_map/concatenate | solution.py:174
  101.1 46.8 %all-gather.8.cloned.1.call-done = bf16[256,8192]{1,0:T(8,128)(2,1)} async-done(((bf16[256,2048]{1,0:T(8,128)(2,1)}), bf16[256,8192]{1,0:T(8,128)(2,1)}) %all-gather.8.cloned.1.call-update) | async-done | bytes 4194320 | tf_op jit(solution)/shard_map/all_gather | solution.py:163
  147.8 18.2 %convolution_convert_fusion.1.cot_ref = bf16[256,2048]{1,0:T(8,128)(2,1)} fusion(bf16[256,8192]{1,0:T(8,128)(2,1)} %all-gather.8.cloned.1.call-done, bf16[2048,8192]{1,0:T(8,128)(2,1)} %refs_0_.1), kind=kOutput, calls=%fused_computation.3 | convolution fusion | flops 8590458880 | bytes 38797312 | tf_op jit(solution)/shard_map/dot_general | solution.py:205
  166.1 131.5 %all-gather.6.cloned.1.call-done = bf16[512,8192]{1,0:T(8,128)(2,1)} async-done(((bf16[512,2048]{1,0:T(8,128)(2,1)}), bf16[512,8192]{1,0:T(8,128)(2,1)}) %all-gather.6.cloned.1.call-update) | async-done | bytes 8388624 | tf_op jit(solution)/shard_map/all_gather | solution.py:163
  297.6 24.8 %convolution_convert_fusion.cot_ref = bf16[512,2048]{1,0:T(8,128)(2,1)} fusion(bf16[512,8192]{1,0:T(8,128)(2,1)} %all-gather.6.cloned.1.call-done, bf16[2048,8192]{1,0:T(8,128)(2,1)} %refs_0_.1), kind=kOutput, calls=%fused_computation.2 | convolution fusion | flops 17180917760 | bytes 44040192 | tf_op jit(solution)/shard_map/dot_general | solution.py:205
  322.4 22.6 %attention_level.4 = (bf16[4,1,256,2048]{3,2,1,0:T(8,128)(2,1)}, f32[4,256,256]{2,1,0:T(8,128)}, f32[4,256,256]{2,1,0:T(8,128)}) custom-call(s32[8]{0:T(128)S(1)} %stack.49.info_ref, bf16[4,1,256,2048]{3,2,1,0:T(8,128)(2,1)} %q_ref.7, bf16[512,2048]{1,0:T(8,128)(2,1)} %convolution_convert_fusion.cot_ref, ...), custom_call_target="tpu_custom_call" | custom-call | flops 21474836480 | bytes 3145728 | tf_op jit(solution)/shard_map/attention_level/pallas_call | solution.py:129
  344.9 1.3 fusion.17
  346.8 18.4 %attention_level.5 = (bf16[4,1,256,2048]{3,2,1,0:T(8,128)(2,1)}, f32[3,256,256]{2,1,0:T(8,128)S(1)}, f32[3,256,256]{2,1,0:T(8,128)}) custom-call(s32[8]{0:T(128)S(1)} %stack.103.info_ref, bf16[4,1,256,2048]{3,2,1,0:T(8,128)(2,1)} %q_ref.7, bf16[512,2048]{1,0:T(8,128)(2,1)} %convolution_convert_fusion.cot_ref, ...), custom_call_target="tpu_custom_call", output_to_operand_aliasing={{0}: (9, {})} | custom-call | flops 16106127360 | bytes 3145728 | tf_op jit(solution)/shard_map/attention_level/pallas_call | solution.py:129
  365.3 1.0 copy-done.5
  366.4 13.9 %attention_level.6 = (bf16[4,1,256,2048]{3,2,1,0:T(8,128)(2,1)}, f32[2,256,256]{2,1,0:T(8,128)S(1)}, f32[2,256,256]{2,1,0:T(8,128)S(1)}) custom-call(s32[8]{0:T(128)S(1)} %stack.106.info_ref, bf16[4,1,256,2048]{3,2,1,0:T(8,128)(2,1)} %q_ref.7, bf16[256,2048]{1,0:T(8,128)(2,1)} %convolution_convert_fusion.1.cot_ref, ...), custom_call_target="tpu_custom_call", output_to_operand_aliasing={{0}: (7, {})} | custom-call | flops 10737418240 | bytes 3145728 | tf_op jit(solution)/shard_map/attention_level/pallas_call | solution.py:129
  380.4 0.5 add_convert_fusion.1
  380.9 0.6 collective-permute-start.3
  381.5 0.4 add_convert_fusion
  382.0 1.0 slice.258
  383.0 0.3 convert_add_fusion
  383.4 1.5 collective-permute-start.10
  384.9 0.6 fusion.16
  385.6 0.6 collective-permute-start.4
  386.2 0.5 fusion.15
  386.7 1.5 collective-permute-start.7
  388.2 9.9 %collective-permute-done.10 = bf16[2,2,256,256]{3,2,1,0:T(8,128)(2,1)S(1)} collective-permute-done((bf16[2,2,256,256]{3,2,1,0:T(8,128)(2,1)S(1)}, bf16[2,2,256,256]{3,2,1,0:T(8,128)(2,1)S(1)}, u32[]{:S(2)}, u32[]{:S(2)}) %collective-permute-start.10) | collective-permute-done | bytes 524320 | tf_op jit(solution)/shard_map/ppermute | solution.py:156
  398.4 1.5 collective-permute-start.11
  399.9 9.5 %collective-permute-done.4 = bf16[2,2,256,256]{3,2,1,0:T(8,128)(2,1)S(1)} collective-permute-done((bf16[2,2,256,256]{3,2,1,0:T(8,128)(2,1)S(1)}, bf16[2,2,256,256]{3,2,1,0:T(8,128)(2,1)S(1)}, u32[]{:S(2)}, u32[]{:S(2)}) %collective-permute-start.4) | collective-permute-done | bytes 524320 | tf_op jit(solution)/shard_map/ppermute | solution.py:156
  409.6 1.5 collective-permute-start.5
  411.1 9.1 %collective-permute-done.7 = bf16[2,2,256,256]{3,2,1,0:T(8,128)(2,1)S(1)} collective-permute-done((bf16[2,2,256,256]{3,2,1,0:T(8,128)(2,1)S(1)}, bf16[2,2,256,256]{3,2,1,0:T(8,128)(2,1)S(1)}, u32[]{:S(2)}, u32[]{:S(2)}) %collective-permute-start.7) | collective-permute-done | bytes 524320 | tf_op jit(solution)/shard_map/ppermute | solution.py:156
  420.4 1.5 collective-permute-start.8
  422.1 6.3 %collective-permute-done.8 = bf16[1,2,256,256]{3,2,1,0:T(8,128)(2,1)S(1)} collective-permute-done((bf16[1,2,256,256]{3,2,1,0:T(8,128)(2,1)S(1)}, bf16[1,2,256,256]{3,2,1,0:T(8,128)(2,1)S(1)}, u32[]{:S(2)}, u32[]{:S(2)}) %collective-permute-start.8) | collective-permute-done | bytes 262176 | tf_op jit(solution)/shard_map/ppermute | solution.py:156
  428.5 21.8 %attention_level.7 = (bf16[4,1,256,2048]{3,2,1,0:T(8,128)(2,1)}, f32[1,256,256]{2,1,0:T(8,128)S(1)}, f32[1,256,256]{2,1,0:T(8,128)S(1)}) custom-call(s32[8]{0:T(128)S(1)} %stack.44.info_ref, bf16[4,1,256,2048]{3,2,1,0:T(8,128)(2,1)} %q_ref.7, bf16[256,8192]{1,0:T(8,128)(2,1)} %all-gather.4.cloned.1.call-done.cot_ref, ...), custom_call_target="tpu_custom_call", output_to_operand_aliasing={{0}: (6, {})} | custom-call | flops 13958643712 | bytes 3145728 | tf_op jit(solution)/shard_map/attention_level/pallas_call | solution.py:129
  450.5 0.9 maximum_bitcast_fusion.2
  451.4 0.9 maximum_bitcast_fusion.1
  (72 shorter events, 2.5 us)
Async XLA Ops:
  7.2 140.7 %all-gather.8.cloned.1.call-start = ((), (), s32[]{:S(2)}) async-start(), calls=%async_computation.2 | async-start | bytes 5242880 | tf_op jit(solution)/shard_map/all_gather | solution.py:163
  9.3 22.6 %copy-start.3 = (bf16[4,1,256,2048]{3,2,1,0:T(8,128)(2,1)S(1)}, bf16[4,1,256,2048]{3,2,1,0:T(8,128)(2,1)}, u32[]{:S(2)}) copy-start(bf16[4,1,256,2048]{3,2,1,0:T(8,128)(2,1)} %param.22) | copy-start | bytes 12582916
  9.4 20.6 %collective-permute-start = (bf16[1,3,2,256,256]{4,3,2,1,0:T(8,128)(2,1)S(1)}, bf16[1,3,2,256,256]{4,3,2,1,0:T(8,128)(2,1)S(1)}, u32[]{:S(2)}, u32[]{:S(2)}) collective-permute-start(bf16[1,3,2,256,256]{4,3,2,1,0:T(8,128)(2,1)S(1)} %maximum_bitcast_fusion), channel_id=1, source_target_pairs={{0,16},{4,20},{8,24},{12,28},{16,0},{20,4},{24,8},{28,12},{1,17},{... | collective-permute-start | bytes 2359304 | tf_op jit(solution)/shard_map/ppermute | solution.py:156
  30.1 35.6 %collective-permute-start.1 = (bf16[2,3,2,256,256]{4,3,2,1,0:T(8,128)(2,1)S(1)}, bf16[2,3,2,256,256]{4,3,2,1,0:T(8,128)(2,1)S(1)}, u32[]{:S(2)}, u32[]{:S(2)}) collective-permute-start(bf16[2,3,2,256,256]{4,3,2,1,0:T(8,128)(2,1)S(1)} %pad_maximum_fusion.2), channel_id=1, source_target_pairs={{0,8},{4,12},{8,0},{12,4},{16,24},{20,28},{24,16},{28,20},{1,9},{5... | collective-permute-start | bytes 4718600 | tf_op jit(solution)/shard_map/ppermute | solution.py:156
  65.8 231.8 %all-gather.6.cloned.1.call-start = ((), (), s32[]{:S(2)}) async-start(), calls=%async_computation.1 | async-start | bytes 10485760 | tf_op jit(solution)/shard_map/all_gather | solution.py:163
  69.0 2.1 copy-start.7
  69.0 19.2 %copy-start.6 = (s32[4,8]{1,0:T(4,128)S(1)}, s32[4,8]{1,0:T(4,128)}, u32[]{:S(2)}) copy-start(s32[4,8]{1,0:T(4,128)} %param.25) | copy-start | bytes 388
  69.0 26.9 %copy-start.8 = (s32[4]{0:T(128)S(1)}, s32[4]{0:T(128)}, u32[]{:S(2)}) copy-start(s32[4]{0:T(128)} %constant.86.clone) | copy-start | bytes 52
  69.0 359.5 %all-gather.4.cloned.1.call-start = ((), (), s32[]{:S(2)}) async-start(), calls=%async_computation | async-start | bytes 5242880 | tf_op jit(solution)/shard_map/all_gather | solution.py:163
  71.0 24.9 %collective-permute-start.2 = (bf16[4,3,2,256,256]{4,3,2,1,0:T(8,128)(2,1)}, bf16[4,3,2,256,256]{4,3,2,1,0:T(8,128)(2,1)}, u32[]{:S(2)}, u32[]{:S(2)}) collective-permute-start(bf16[4,3,2,256,256]{4,3,2,1,0:T(8,128)(2,1)} %pad_maximum_fusion.1), channel_id=1, source_target_pairs={{0,4},{4,0},{8,12},{12,8},{16,20},{20,16},{24,28},{28,24},{1,5},{5... | collective-permute-start | bytes 9437192 | tf_op jit(solution)/shard_map/ppermute | solution.py:156
  166.1 156.3 %copy-start = (bf16[4,1,256,256]{3,2,1,0:T(8,128)(2,1)S(1)}, bf16[4,1,256,256]{3,2,1,0:T(8,128)(2,1)}, u32[]{:S(2)}) copy-start(bf16[4,1,256,256]{3,2,1,0:T(8,128)(2,1)} %refs_1_.3) | copy-start | bytes 1572868
  166.1 156.3 %copy-start.1 = (bf16[4,1,256,256]{3,2,1,0:T(8,128)(2,1)S(1)}, bf16[4,1,256,256]{3,2,1,0:T(8,128)(2,1)}, u32[]{:S(2)}) copy-start(bf16[4,1,256,256]{3,2,1,0:T(8,128)(2,1)} %refs_2_.3) | copy-start | bytes 1572868
  344.9 1.5 copy-start.4
  346.7 36.3 %collective-permute-start.9 = (bf16[4,2,256,256]{3,2,1,0:T(8,128)(2,1)S(1)}, bf16[4,2,256,256]{3,2,1,0:T(8,128)(2,1)S(1)}, u32[]{:S(2)}, u32[]{:S(2)}) collective-permute-start(bf16[4,2,256,256]{3,2,1,0:T(8,128)(2,1)S(1)} %select_convert_fusion), channel_id=1, source_target_pairs={{0,4},{4,0},{8,12},{12,8},{16,20},{20,16},{24,28},{28,24},{1,5},{5... | collective-permute-start | bytes 3145736 | tf_op jit(solution)/shard_map/ppermute | solution.py:156
  365.2 1.1 copy-start.5
  380.9 4.0 collective-permute-start.3
  381.9 4.3 collective-permute-start.6
  383.4 14.8 %collective-permute-start.10 = (bf16[2,2,256,256]{3,2,1,0:T(8,128)(2,1)S(1)}, bf16[2,2,256,256]{3,2,1,0:T(8,128)(2,1)S(1)}, u32[]{:S(2)}, u32[]{:S(2)}) collective-permute-start(bf16[2,2,256,256]{3,2,1,0:T(8,128)(2,1)S(1)} %slice.206), channel_id=1, source_target_pairs={{0,8},{4,12},{8,0},{12,4},{16,24},{20,28},{24,16},{28,20},{1,9},{5... | collective-permute-start | bytes 1572872 | tf_op jit(solution)/shard_map/ppermute | solution.py:156
  385.6 23.9 %collective-permute-start.4 = (bf16[2,2,256,256]{3,2,1,0:T(8,128)(2,1)S(1)}, bf16[2,2,256,256]{3,2,1,0:T(8,128)(2,1)S(1)}, u32[]{:S(2)}, u32[]{:S(2)}) collective-permute-start(bf16[2,2,256,256]{3,2,1,0:T(8,128)(2,1)S(1)} %slice.192), channel_id=1, source_target_pairs={{0,8},{4,12},{8,0},{12,4},{16,24},{20,28},{24,16},{28,20},{1,9},{5... | collective-permute-start | bytes 1572872 | tf_op jit(solution)/shard_map/ppermute | solution.py:156
  386.7 33.5 %collective-permute-start.7 = (bf16[2,2,256,256]{3,2,1,0:T(8,128)(2,1)S(1)}, bf16[2,2,256,256]{3,2,1,0:T(8,128)(2,1)S(1)}, u32[]{:S(2)}, u32[]{:S(2)}) collective-permute-start(bf16[2,2,256,256]{3,2,1,0:T(8,128)(2,1)S(1)} %slice.200), channel_id=1, source_target_pairs={{0,8},{4,12},{8,0},{12,4},{16,24},{20,28},{24,16},{28,20},{1,9},{5... | collective-permute-start | bytes 1572872 | tf_op jit(solution)/shard_map/ppermute | solution.py:156
  398.4 23.6 %collective-permute-start.11 = (bf16[1,2,256,256]{3,2,1,0:T(8,128)(2,1)S(1)}, bf16[1,2,256,256]{3,2,1,0:T(8,128)(2,1)S(1)}, u32[]{:S(2)}, u32[]{:S(2)}) collective-permute-start(bf16[1,2,256,256]{3,2,1,0:T(8,128)(2,1)S(1)} %slice.254), channel_id=1, source_target_pairs={{0,16},{4,20},{8,24},{12,28},{16,0},{20,4},{24,8},{28,12},{1,17},{... | collective-permute-start | bytes 786440 | tf_op jit(solution)/shard_map/ppermute | solution.py:156
  409.6 12.3 %collective-permute-start.5 = (bf16[1,2,256,256]{3,2,1,0:T(8,128)(2,1)S(1)}, bf16[1,2,256,256]{3,2,1,0:T(8,128)(2,1)S(1)}, u32[]{:S(2)}, u32[]{:S(2)}) collective-permute-start(bf16[1,2,256,256]{3,2,1,0:T(8,128)(2,1)S(1)} %slice.256), channel_id=1, source_target_pairs={{0,16},{4,20},{8,24},{12,28},{16,0},{20,4},{24,8},{28,12},{1,17},{... | collective-permute-start | bytes 786440 | tf_op jit(solution)/shard_map/ppermute | solution.py:156
  420.4 8.1 %copy-start.2 = (bf16[4,1,256,256]{3,2,1,0:T(8,128)(2,1)S(1)}, bf16[4,1,256,256]{3,2,1,0:T(8,128)(2,1)}, u32[]{:S(2)}) copy-start(bf16[4,1,256,256]{3,2,1,0:T(8,128)(2,1)} %refs_2_.3) | copy-start | bytes 1572868
  420.4 8.0 %collective-permute-start.8 = (bf16[1,2,256,256]{3,2,1,0:T(8,128)(2,1)S(1)}, bf16[1,2,256,256]{3,2,1,0:T(8,128)(2,1)S(1)}, u32[]{:S(2)}, u32[]{:S(2)}) collective-permute-start(bf16[1,2,256,256]{3,2,1,0:T(8,128)(2,1)S(1)} %slice.255), channel_id=1, source_target_pairs={{0,16},{4,20},{8,24},{12,28},{16,0},{20,4},{24,8},{28,12},{1,17},{... | collective-permute-start | bytes 786440 | tf_op jit(solution)/shard_map/ppermute | solution.py:156
Sparse Core Ops, SparseCore 0:
  65.9 81.9 all-gather.7
  149.4 148.1 all-gather.5
  299.2 78.9 all-gather.3

commit v4 on v3

--- a/solution.py
+++ b/solution.py
@@ -156,22 +156,15 @@
         return lax.ppermute(array, "branch", pairs)
 
     width = cotangent.shape[3]
+    chunks = [(levels - 2, levels)] + [(m, m + 1) for m in reversed(range(levels - 2))]
     gathered = {}
-
-    def gather(first, last, rows):
-        rows = rows.reshape((last - first) * seg, width)
+    for first, last in chunks:
+        rows = cotangent[first:last, 0].reshape((last - first) * seg, width)
         gathered[first] = lax.all_gather(rows, "head", axis=1, tiled=True)
 
-    gather(levels - 2, levels, cotangent[levels - 2 :, 0])
     kv_all = jnp.stack([key_rows[: levels - 1, 0], value_rows[: levels - 1, 0]], axis=1)[None]
-    waiting = list(range(levels - 2))
     for bit in reversed(range(bits)):
-        arrived = swap(kv_all, bit)
-        if bit < len(waiting):
-            level = waiting.pop()
-            rows, arrived = lax.optimization_barrier((cotangent[level, 0], arrived))
-            gather(level, level + 1, rows)
-        kv_all = jnp.concatenate([kv_all, arrived], axis=0)
+        kv_all = jnp.concatenate([kv_all, swap(kv_all, bit)], axis=0)
 
     offsets = []
     infos = []
@@ -198,6 +191,8 @@
         first = min(level, levels - 2)
         if level == 0:
             gathered[0], *received = lax.optimization_barrier((gathered[0], *received))
+        elif level < levels - 2:
+            gathered[level], dk = lax.optimization_barrier((gathered[level], dk))
         if level == 0:
             cot, weight = gathered[0], out_weight
         else:

time: 460 us -> 358 us (0.78)
  waiting for transfers between devices: 263 us -> 155 us
    all_gather x3, waiting for transfers between devices: 178 us -> 68.6 us  [local(): gathered[first] = lax.all_gather(rows, 'head', axis=1, tiled=True)]
  transfers between devices with their start and end apart: 15 -> 15, of which waited for: 8 -> 8; matrix products, arithmetic and copies ran while one was open for 15% -> 21% of each run, Pallas kernels for 12% -> 15%
where the time goes in v4:
time: 358 us; the launch traced here: 357 us
  waiting for transfers between devices  155 us (43%)
  Pallas kernels  76.3 us (21%)
  matrix products  42.2 us (12%)
  between operations  29.7 us (8%)
  local copies, waits for them, and re-layouts  24.5 us (7%)
  other arithmetic  15.5 us (4%)
  starting transfers between devices  13.6 us (4%)
    ppermute x12, waiting for transfers between devices, swap(): return lax.ppermute(array, 'branch', pairs)  86.3 us
    pallas_call x4, Pallas kernels, attention_level(): pl.pallas_call(functools.partial(attention_kernel, level, fused, int(base...  76.3 us
    all_gather x3, waiting for transfers between devices, local(): gathered[first] = lax.all_gather(rows, 'head', axis=1, tiled=True)  68.6 us
    dot_general x2, matrix products, local(): lax.dot_general(gathered[first], out_weight, NT, preferred_element_type=j...  42.2 us
    ppermute x12, starting transfers between devices, swap(): return lax.ppermute(array, 'branch', pairs)  13.4 us
    concatenate x3, other arithmetic, local(): kv_all = jnp.concatenate([kv_all, swap(kv_all, bit)], axis=0)  8.17 us
  transfers between devices with their start and end apart: 15, of which 8 were waited for; matrix products, arithmetic and copies ran while one was open for 21% of the time, Pallas kernels for 15%

profile of v4, /device:TPU:0, one launch (start us, length us, event | category | flops | bytes accessed | tf_op | source)
XLA Modules:
  0.0 356.8 jit_solution(14401193586184470946)
XLA Ops:
  7.2 3.1 slice.181
  10.4 3.1 fusion.17
  13.6 0.9 slice-done
  14.7 3.0 collective-permute-start
  17.7 17.5 %collective-permute-done = bf16[1,3,2,256,256]{4,3,2,1,0:T(8,128)(2,1)S(1)} collective-permute-done((bf16[1,3,2,256,256]{4,3,2,1,0:T(8,128)(2,1)S(1)}, bf16[1,3,2,256,256]{4,3,2,1,0:T(8,128)(2,1)S(1)}, u32[]{:S(2)}, u32[]{:S(2)}) %collective-permute-start) | collective-permute-done | bytes 786464 | tf_op jit(solution)/shard_map/ppermute | solution.py:156
  35.5 1.8 collective-permute-start.1
  37.2 34.0 %collective-permute-done.1 = bf16[2,3,2,256,256]{4,3,2,1,0:T(8,128)(2,1)S(1)} collective-permute-done((bf16[2,3,2,256,256]{4,3,2,1,0:T(8,128)(2,1)S(1)}, bf16[2,3,2,256,256]{4,3,2,1,0:T(8,128)(2,1)S(1)}, u32[]{:S(2)}, u32[]{:S(2)}) %collective-permute-start.1) | collective-permute-done | bytes 1572896 | tf_op jit(solution)/shard_map/ppermute | solution.py:156
  71.2 2.2 pad_maximum_fusion.1
  73.5 0.6 constant_dynamic-slice_fusion.14
  76.0 0.6 constant_dynamic-slice_fusion.13
  81.1 0.7 constant_dynamic-slice_fusion.12
  91.0 0.7 constant_dynamic-slice_fusion.10
  91.6 0.7 stack.44.info_ref
  92.3 1.4 stack.106.info_ref
  93.8 0.7 constant_dynamic-slice_fusion.9
  94.4 2.0 stack.103.info_ref
  96.4 2.7 stack.48.info_ref
  99.1 5.8 %pad_maximum_fusion.refs_0_.refs_1_.refs_2_.refs_4_.refs_5_.refs_6_.refs_3_ = bf16[8,3,2,256,256]{4,3,2,1,0:T(8,128)(2,1)} fusion(bf16[4,3,2,256,256]{4,3,2,1,0:T(8,128)(2,1)} %collective-permute-done.2, bf16[2,3,2,256,256]{4,3,2,1,0:T(8,128)(2,1)} %copy-done.3, bf16[1,3,2,256,256]{4,3,2,1,0:T(8,128)(2,1)S(1)} %collective-permute-done, ...), kind=kLoop, calls=%fused_computation | loop fusion | flops 9437184 | bytes 12582912 | tf_op jit(solution)/shard_map/concatenate | solution.py:167
  105.0 57.9 %all-gather.6.cloned.1.call-done = bf16[512,8192]{1,0:T(8,128)(2,1)} async-done(((bf16[512,2048]{1,0:T(8,128)(2,1)}), bf16[512,8192]{1,0:T(8,128)(2,1)}) %all-gather.6.cloned.1.call-update) | async-done | bytes 8388624 | tf_op jit(solution)/shard_map/all_gather | solution.py:163
  162.9 24.7 %convolution_convert_fusion.cot_ref = bf16[512,2048]{1,0:T(8,128)(2,1)} fusion(bf16[512,8192]{1,0:T(8,128)(2,1)} %all-gather.6.cloned.1.call-done, bf16[2048,8192]{1,0:T(8,128)(2,1)} %refs_0_.1), kind=kOutput, calls=%fused_computation.2 | convolution fusion | flops 17180917760 | bytes 44040192 | tf_op jit(solution)/shard_map/dot_general | solution.py:200
  187.6 22.5 %attention_level.4 = (bf16[4,1,256,2048]{3,2,1,0:T(8,128)(2,1)}, f32[4,256,256]{2,1,0:T(8,128)}, f32[4,256,256]{2,1,0:T(8,128)}) custom-call(s32[8]{0:T(128)S(1)} %stack.48.info_ref, bf16[4,1,256,2048]{3,2,1,0:T(8,128)(2,1)} %q_ref.7, bf16[512,2048]{1,0:T(8,128)(2,1)} %convolution_convert_fusion.cot_ref, ...), custom_call_target="tpu_custom_call" | custom-call | flops 21474836480 | bytes 3145728 | tf_op jit(solution)/shard_map/attention_level/pallas_call | solution.py:129
  210.2 2.0 fusion.18
  212.2 0.8 fusion.19
  213.1 1.2 select_convert_fusion
  214.3 18.3 %attention_level.5 = (bf16[4,1,256,2048]{3,2,1,0:T(8,128)(2,1)}, f32[3,256,256]{2,1,0:T(8,128)S(1)}, f32[3,256,256]{2,1,0:T(8,128)}) custom-call(s32[8]{0:T(128)S(1)} %stack.103.info_ref, bf16[4,1,256,2048]{3,2,1,0:T(8,128)(2,1)} %q_ref.7, bf16[512,2048]{1,0:T(8,128)(2,1)} %convolution_convert_fusion.cot_ref, ...), custom_call_target="tpu_custom_call", output_to_operand_aliasing={{0}: (9, {})} | custom-call | flops 16106127360 | bytes 3145728 | tf_op jit(solution)/shard_map/attention_level/pallas_call | solution.py:129
  232.7 10.7 %all-gather.10.cloned.1.call-done = bf16[1,1,256,8192]{3,2,1,0:T(8,128)(2,1)} async-done(((bf16[1,1,256,2048]{3,2,1,0:T(8,128)(2,1)}), bf16[1,1,256,8192]{3,2,1,0:T(8,128)(2,1)}) %all-gather.10.cloned.1.call-update) | async-done | bytes 4194320 | tf_op jit(solution)/shard_map/all_gather | solution.py:163
  243.4 17.4 %convolution_convert_fusion.1.cot_ref = bf16[256,2048]{1,0:T(8,128)(2,1)} fusion(bf16[256,8192]{1,0:T(8,128)(2,1)} %bitcast.49, bf16[2048,8192]{1,0:T(8,128)(2,1)} %refs_0_.1), kind=kOutput, calls=%fused_computation.3 | convolution fusion | flops 8590458880 | bytes 38797312 | tf_op jit(solution)/shard_map/dot_general | solution.py:200
  260.8 1.1 pad_maximum_fusion.3
  262.2 13.9 %attention_level.6 = (bf16[4,1,256,2048]{3,2,1,0:T(8,128)(2,1)}, f32[2,256,256]{2,1,0:T(8,128)S(1)}, f32[2,256,256]{2,1,0:T(8,128)S(1)}) custom-call(s32[8]{0:T(128)S(1)} %stack.106.info_ref, bf16[4,1,256,2048]{3,2,1,0:T(8,128)(2,1)} %q_ref.7, bf16[256,2048]{1,0:T(8,128)(2,1)} %convolution_convert_fusion.1.cot_ref, ...), custom_call_target="tpu_custom_call", output_to_operand_aliasing={{0}: (7, {})} | custom-call | flops 10737418240 | bytes 3145728 | tf_op jit(solution)/shard_map/attention_level/pallas_call | solution.py:129
  276.2 0.5 add_convert_fusion.1
  277.8 1.6 slice.255
  279.5 1.0 slice.256
  280.9 1.5 collective-permute-start.10
  282.4 0.6 fusion.16
  283.1 0.6 collective-permute-start.4
  283.7 0.5 fusion.15
  284.2 1.5 collective-permute-start.7
  285.7 9.9 %collective-permute-done.10 = bf16[2,2,256,256]{3,2,1,0:T(8,128)(2,1)S(1)} collective-permute-done((bf16[2,2,256,256]{3,2,1,0:T(8,128)(2,1)S(1)}, bf16[2,2,256,256]{3,2,1,0:T(8,128)(2,1)S(1)}, u32[]{:S(2)}, u32[]{:S(2)}) %collective-permute-start.10) | collective-permute-done | bytes 524320 | tf_op jit(solution)/shard_map/ppermute | solution.py:156
  295.8 1.5 collective-permute-start.11
  297.4 9.5 %collective-permute-done.4 = bf16[2,2,256,256]{3,2,1,0:T(8,128)(2,1)S(1)} collective-permute-done((bf16[2,2,256,256]{3,2,1,0:T(8,128)(2,1)S(1)}, bf16[2,2,256,256]{3,2,1,0:T(8,128)(2,1)S(1)}, u32[]{:S(2)}, u32[]{:S(2)}) %collective-permute-start.4) | collective-permute-done | bytes 524320 | tf_op jit(solution)/shard_map/ppermute | solution.py:156
  307.1 1.5 collective-permute-start.5
  308.6 9.0 %collective-permute-done.7 = bf16[2,2,256,256]{3,2,1,0:T(8,128)(2,1)S(1)} collective-permute-done((bf16[2,2,256,256]{3,2,1,0:T(8,128)(2,1)S(1)}, bf16[2,2,256,256]{3,2,1,0:T(8,128)(2,1)S(1)}, u32[]{:S(2)}, u32[]{:S(2)}) %collective-permute-start.7) | collective-permute-done | bytes 524320 | tf_op jit(solution)/shard_map/ppermute | solution.py:156
  317.9 1.5 collective-permute-start.8
  319.6 6.3 %collective-permute-done.8 = bf16[1,2,256,256]{3,2,1,0:T(8,128)(2,1)S(1)} collective-permute-done((bf16[1,2,256,256]{3,2,1,0:T(8,128)(2,1)S(1)}, bf16[1,2,256,256]{3,2,1,0:T(8,128)(2,1)S(1)}, u32[]{:S(2)}, u32[]{:S(2)}) %collective-permute-start.8) | collective-permute-done | bytes 262176 | tf_op jit(solution)/shard_map/ppermute | solution.py:156
  326.0 21.6 %attention_level.7 = (bf16[4,1,256,2048]{3,2,1,0:T(8,128)(2,1)}, f32[1,256,256]{2,1,0:T(8,128)S(1)}, f32[1,256,256]{2,1,0:T(8,128)S(1)}) custom-call(s32[8]{0:T(128)S(1)} %stack.44.info_ref, bf16[4,1,256,2048]{3,2,1,0:T(8,128)(2,1)} %q_ref.7, bf16[256,8192]{1,0:T(8,128)(2,1)} %bitcast.48, ...), custom_call_target="tpu_custom_call", output_to_operand_aliasing={{0}: (6, {})} | custom-call | flops 13958643712 | bytes 3145728 | tf_op jit(solution)/shard_map/attention_level/pallas_call | solution.py:129
  347.8 0.7 copy-done.8
  348.5 0.9 maximum_bitcast_fusion.2
  349.4 0.9 maximum_bitcast_fusion.1
  (80 shorter events, 3.5 us)
Async XLA Ops:
  7.2 155.7 %all-gather.6.cloned.1.call-start = ((), (), s32[]{:S(2)}) async-start(), calls=%async_computation | async-start | bytes 10485760 | tf_op jit(solution)/shard_map/all_gather | solution.py:163
  10.4 233.0 %all-gather.10.cloned.1.call-start = ((), (), s32[]{:S(2)}) async-start(), calls=%async_computation.2 | async-start | bytes 5242880 | tf_op jit(solution)/shard_map/all_gather | solution.py:163
  13.5 1.0 slice-start
  13.5 1.1 slice-start.1
  13.5 312.5 %all-gather.8.cloned.1.call-start = ((), (), s32[]{:S(2)}) async-start(), calls=%async_computation.1 | async-start | bytes 5242880 | tf_op jit(solution)/shard_map/all_gather | solution.py:163
  14.7 20.6 %collective-permute-start = (bf16[1,3,2,256,256]{4,3,2,1,0:T(8,128)(2,1)S(1)}, bf16[1,3,2,256,256]{4,3,2,1,0:T(8,128)(2,1)S(1)}, u32[]{:S(2)}, u32[]{:S(2)}) collective-permute-start(bf16[1,3,2,256,256]{4,3,2,1,0:T(8,128)(2,1)S(1)} %maximum_bitcast_fusion), channel_id=1, source_target_pairs={{0,16},{4,20},{8,24},{12,28},{16,0},{20,4},{24,8},{28,12},{1,17},{... | collective-permute-start | bytes 2359304 | tf_op jit(solution)/shard_map/ppermute | solution.py:156
  35.4 38.0 %copy-start.10 = (s32[3,8]{1,0:T(4,128)S(1)}, s32[3,8]{1,0:T(4,128)}, u32[]{:S(2)}) copy-start(s32[3,8]{1,0:T(4,128)} %param.24) | copy-start | bytes 292
  35.4 55.5 %copy-start.9 = (s32[4,8]{1,0:T(4,128)S(1)}, s32[4,8]{1,0:T(4,128)}, u32[]{:S(2)}) copy-start(s32[4,8]{1,0:T(4,128)} %param.25) | copy-start | bytes 388
  35.5 63.6 %copy-start.11 = (s32[4]{0:T(128)S(1)}, s32[4]{0:T(128)}, u32[]{:S(2)}) copy-start(s32[4]{0:T(128)} %constant.86.clone) | copy-start | bytes 52
  35.5 35.8 %collective-permute-start.1 = (bf16[2,3,2,256,256]{4,3,2,1,0:T(8,128)(2,1)S(1)}, bf16[2,3,2,256,256]{4,3,2,1,0:T(8,128)(2,1)S(1)}, u32[]{:S(2)}, u32[]{:S(2)}) collective-permute-start(bf16[2,3,2,256,256]{4,3,2,1,0:T(8,128)(2,1)S(1)} %pad_maximum_fusion.2), channel_id=1, source_target_pairs={{0,8},{4,12},{8,0},{12,4},{16,24},{20,28},{24,16},{28,20},{1,9},{5... | collective-permute-start | bytes 4718600 | tf_op jit(solution)/shard_map/ppermute | solution.py:156
  71.2 2.2 copy-start.3
  73.4 25.7 %collective-permute-start.2 = (bf16[4,3,2,256,256]{4,3,2,1,0:T(8,128)(2,1)}, bf16[4,3,2,256,256]{4,3,2,1,0:T(8,128)(2,1)}, u32[]{:S(2)}, u32[]{:S(2)}) collective-permute-start(bf16[4,3,2,256,256]{4,3,2,1,0:T(8,128)(2,1)} %pad_maximum_fusion.1), channel_id=1, source_target_pairs={{0,4},{4,0},{8,12},{12,8},{16,20},{20,16},{24,28},{28,24},{1,5},{5... | collective-permute-start | bytes 9437192 | tf_op jit(solution)/shard_map/ppermute | solution.py:156
  105.0 82.6 %copy-start = (bf16[4,1,256,256]{3,2,1,0:T(8,128)(2,1)S(1)}, bf16[4,1,256,256]{3,2,1,0:T(8,128)(2,1)}, u32[]{:S(2)}) copy-start(bf16[4,1,256,256]{3,2,1,0:T(8,128)(2,1)} %refs_1_.3) | copy-start | bytes 1572868
  105.0 82.6 %copy-start.1 = (bf16[4,1,256,256]{3,2,1,0:T(8,128)(2,1)S(1)}, bf16[4,1,256,256]{3,2,1,0:T(8,128)(2,1)}, u32[]{:S(2)}) copy-start(bf16[4,1,256,256]{3,2,1,0:T(8,128)(2,1)} %refs_2_.3) | copy-start | bytes 1572868
  210.2 2.1 copy-start.6
  214.3 66.2 %collective-permute-start.9 = (bf16[4,2,256,256]{3,2,1,0:T(8,128)(2,1)}, bf16[4,2,256,256]{3,2,1,0:T(8,128)(2,1)S(1)}, u32[]{:S(2)}, u32[]{:S(2)}) collective-permute-start(bf16[4,2,256,256]{3,2,1,0:T(8,128)(2,1)} %select_convert_fusion), channel_id=1, source_target_pairs={{0,4},{4,0},{8,12},{12,8},{16,20},{20,16},{24,28},{28,24},{1,5},{5... | collective-permute-start | bytes 3145736 | tf_op jit(solution)/shard_map/ppermute | solution.py:156
  260.8 1.3 copy-start.7
  276.2 1.0 copy-start.4
  276.2 1.0 copy-start.5
  276.7 5.7 %collective-permute-start.3 = (bf16[4,2,256,256]{3,2,1,0:T(8,128)(2,1)S(1)}, bf16[4,2,256,256]{3,2,1,0:T(8,128)(2,1)S(1)}, u32[]{:S(2)}, u32[]{:S(2)}) collective-permute-start(bf16[4,2,256,256]{3,2,1,0:T(8,128)(2,1)S(1)} %add_convert_fusion.1), channel_id=1, source_target_pairs={{0,4},{4,0},{8,12},{12,8},{16,20},{20,16},{24,28},{28,24},{1,5},{5... | collective-permute-start | bytes 3145736 | tf_op jit(solution)/shard_map/ppermute | solution.py:156
  277.7 6.0 %collective-permute-start.6 = (bf16[4,2,256,256]{3,2,1,0:T(8,128)(2,1)S(1)}, bf16[4,2,256,256]{3,2,1,0:T(8,128)(2,1)S(1)}, u32[]{:S(2)}, u32[]{:S(2)}) collective-permute-start(bf16[4,2,256,256]{3,2,1,0:T(8,128)(2,1)S(1)} %add_convert_fusion), channel_id=1, source_target_pairs={{0,4},{4,0},{8,12},{12,8},{16,20},{20,16},{24,28},{28,24},{1,5},{5... | collective-permute-start | bytes 3145736 | tf_op jit(solution)/shard_map/ppermute | solution.py:156
  280.9 14.8 %collective-permute-start.10 = (bf16[2,2,256,256]{3,2,1,0:T(8,128)(2,1)S(1)}, bf16[2,2,256,256]{3,2,1,0:T(8,128)(2,1)S(1)}, u32[]{:S(2)}, u32[]{:S(2)}) collective-permute-start(bf16[2,2,256,256]{3,2,1,0:T(8,128)(2,1)S(1)} %slice.206), channel_id=1, source_target_pairs={{0,8},{4,12},{8,0},{12,4},{16,24},{20,28},{24,16},{28,20},{1,9},{5... | collective-permute-start | bytes 1572872 | tf_op jit(solution)/shard_map/ppermute | solution.py:156
  283.1 23.9 %collective-permute-start.4 = (bf16[2,2,256,256]{3,2,1,0:T(8,128)(2,1)S(1)}, bf16[2,2,256,256]{3,2,1,0:T(8,128)(2,1)S(1)}, u32[]{:S(2)}, u32[]{:S(2)}) collective-permute-start(bf16[2,2,256,256]{3,2,1,0:T(8,128)(2,1)S(1)} %slice.192), channel_id=1, source_target_pairs={{0,8},{4,12},{8,0},{12,4},{16,24},{20,28},{24,16},{28,20},{1,9},{5... | collective-permute-start | bytes 1572872 | tf_op jit(solution)/shard_map/ppermute | solution.py:156
  284.2 33.5 %collective-permute-start.7 = (bf16[2,2,256,256]{3,2,1,0:T(8,128)(2,1)S(1)}, bf16[2,2,256,256]{3,2,1,0:T(8,128)(2,1)S(1)}, u32[]{:S(2)}, u32[]{:S(2)}) collective-permute-start(bf16[2,2,256,256]{3,2,1,0:T(8,128)(2,1)S(1)} %slice.200), channel_id=1, source_target_pairs={{0,8},{4,12},{8,0},{12,4},{16,24},{20,28},{24,16},{28,20},{1,9},{5... | collective-permute-start | bytes 1572872 | tf_op jit(solution)/shard_map/ppermute | solution.py:156
  295.8 23.6 %collective-permute-start.11 = (bf16[1,2,256,256]{3,2,1,0:T(8,128)(2,1)S(1)}, bf16[1,2,256,256]{3,2,1,0:T(8,128)(2,1)S(1)}, u32[]{:S(2)}, u32[]{:S(2)}) collective-permute-start(bf16[1,2,256,256]{3,2,1,0:T(8,128)(2,1)S(1)} %slice.252), channel_id=1, source_target_pairs={{0,16},{4,20},{8,24},{12,28},{16,0},{20,4},{24,8},{28,12},{1,17},{... | collective-permute-start | bytes 786440 | tf_op jit(solution)/shard_map/ppermute | solution.py:156
  307.1 12.3 %collective-permute-start.5 = (bf16[1,2,256,256]{3,2,1,0:T(8,128)(2,1)S(1)}, bf16[1,2,256,256]{3,2,1,0:T(8,128)(2,1)S(1)}, u32[]{:S(2)}, u32[]{:S(2)}) collective-permute-start(bf16[1,2,256,256]{3,2,1,0:T(8,128)(2,1)S(1)} %slice.254), channel_id=1, source_target_pairs={{0,16},{4,20},{8,24},{12,28},{16,0},{20,4},{24,8},{28,12},{1,17},{... | collective-permute-start | bytes 786440 | tf_op jit(solution)/shard_map/ppermute | solution.py:156
  317.8 8.2 %copy-start.2 = (bf16[4,1,256,256]{3,2,1,0:T(8,128)(2,1)S(1)}, bf16[4,1,256,256]{3,2,1,0:T(8,128)(2,1)}, u32[]{:S(2)}) copy-start(bf16[4,1,256,256]{3,2,1,0:T(8,128)(2,1)} %refs_2_.3) | copy-start | bytes 1572868
  317.9 8.0 %collective-permute-start.8 = (bf16[1,2,256,256]{3,2,1,0:T(8,128)(2,1)S(1)}, bf16[1,2,256,256]{3,2,1,0:T(8,128)(2,1)S(1)}, u32[]{:S(2)}, u32[]{:S(2)}) collective-permute-start(bf16[1,2,256,256]{3,2,1,0:T(8,128)(2,1)S(1)} %slice.253), channel_id=1, source_target_pairs={{0,16},{4,20},{8,24},{12,28},{16,0},{20,4},{24,8},{28,12},{1,17},{... | collective-permute-start | bytes 786440 | tf_op jit(solution)/shard_map/ppermute | solution.py:156
  347.6 0.9 copy-start.8
Sparse Core Ops, SparseCore 0:
  10.5 152.3 all-gather.5
  164.4 78.9 all-gather.9
  245.0 79.2 all-gather.7

commit v5 on v4

--- a/solution.py
+++ b/solution.py
@@ -21,7 +21,7 @@
 def attention_kernel(level, fused, has_base, info_ref, q_ref, cot_ref, *refs):
     blocks = level + 1
     if fused:
-        weight_ref, refs = refs[0], refs[1:]
+        weight_ref, probs_ref, refs = refs[0], refs[1], refs[2:]
     key_refs, value_refs = refs[:blocks], refs[blocks : 2 * blocks]
     dq_ref, dk_ref, dv_ref = refs[2 * blocks + has_base :]
     seg = cot_ref.shape[0]
@@ -51,17 +51,20 @@
         columns = slice(h * HD, (h + 1) * HD)
         q = q_ref[0, 0, :, columns]
         dout = douts[:, columns]
-        scores = []
-        for m in range(blocks):
-            allowed = key_pos < info_ref[4 + m]
-            if m == level:
-                allowed = allowed & (key_pos <= query_pos)
-            scores.append(jnp.where(allowed, dot(keys[m], q, NT), MASKED))
-        top = functools.reduce(jnp.maximum, [jnp.max(s, axis=0, keepdims=True) for s in scores])
-        exps = [jnp.exp((s - top) * scale) for s in scores]
-        total = functools.reduce(jnp.add, [jnp.sum(e, axis=0, keepdims=True) for e in exps])
-        inverse = 1.0 / total
-        probs = [e * inverse for e in exps]
+        if fused:
+            probs = [probs_ref[h]]
+        else:
+            scores = []
+            for m in range(blocks):
+                allowed = key_pos < info_ref[4 + m]
+                if m == level:
+                    allowed = allowed & (key_pos <= query_pos)
+                scores.append(jnp.where(allowed, dot(keys[m], q, NT), MASKED))
+            top = functools.reduce(jnp.maximum, [jnp.max(s, axis=0, keepdims=True) for s in scores])
+            exps = [jnp.exp((s - top) * scale) for s in scores]
+            total = functools.reduce(jnp.add, [jnp.sum(e, axis=0, keepdims=True) for e in exps])
+            inverse = 1.0 / total
+            probs = [e * inverse for e in exps]
         narrow = [p.astype(jnp.bfloat16) for p in probs]
         dprobs = [dot(v, dout, NT) for v in values]
         delta = functools.reduce(
@@ -80,7 +83,43 @@
         dq_ref[0, 0, :, columns] = (dq * scale).T.astype(jnp.bfloat16)
 
 
-def attention_level(level, row_block, info, queries, cot, weight, key_rows, value_rows, kv_all, base):
+def probs_kernel(info_ref, q_ref, key_ref, probs_ref):
+    seg = q_ref.shape[2]
+    scale = 1.0 / HD**0.5
+    key_pos = lax.broadcasted_iota(jnp.int32, (seg, seg), 0)
+    query_pos = lax.broadcasted_iota(jnp.int32, (seg, seg), 1)
+    allowed = (key_pos < info_ref[4]) & (key_pos <= query_pos)
+    for h in range(probs_ref.shape[0]):
+        q = q_ref[0, 0, :, h * HD : (h + 1) * HD]
+        score = lax.dot_general(key_ref[0, 0], q, NT, preferred_element_type=jnp.float32)
+        score = jnp.where(allowed, score, MASKED)
+        e = jnp.exp((score - jnp.max(score, axis=0, keepdims=True)) * scale)
+        probs_ref[h] = e * (1.0 / jnp.sum(e, axis=0, keepdims=True))
+
+
+def first_probs(info, queries, key_rows):
+    seg, q_width, kv_width = queries.shape[2], queries.shape[3], key_rows.shape[3]
+    kv_local, group = kv_width // HD, q_width // kv_width
+    heads = min(4, group)
+    steps = group // heads
+    return pl.pallas_call(
+        probs_kernel,
+        grid_spec=pltpu.PrefetchScalarGridSpec(
+            num_scalar_prefetch=1,
+            grid=(kv_local, steps),
+            in_specs=[
+                pl.BlockSpec((1, 1, seg, heads * HD), lambda n, g, info: (0, 0, 0, n * steps + g)),
+                pl.BlockSpec((1, 1, seg, HD), lambda n, g, info: (0, 0, 0, n)),
+            ],
+            out_specs=pl.BlockSpec((heads, seg, seg), lambda n, g, info: (n * steps + g, 0, 0)),
+        ),
+        out_shape=jax.ShapeDtypeStruct((kv_local * group, seg, seg), jnp.float32),
+        compiler_params=pltpu.CompilerParams(vmem_limit_bytes=32 * 1024 * 1024),
+        name="first_probs",
+    )(info, queries, key_rows)
+
+
+def attention_level(level, row_block, info, queries, cot, weight, key_rows, value_rows, kv_all, base, probs):
     levels, _, seg, q_width = queries.shape
     kv_width = key_rows.shape[3]
     kv_local = kv_width // HD
@@ -105,8 +144,9 @@
         cot_specs = [
             pl.BlockSpec((seg, model), lambda n, g, info: (row_block, 0)),
             pl.BlockSpec((heads * HD, model), lambda n, g, info: (n * steps + g, 0)),
+            pl.BlockSpec((heads, seg, seg), lambda n, g, info: (n * steps + g, 0, 0)),
         ]
-        cots = [cot, weight]
+        cots = [cot, weight, probs]
     else:
         products_in = 0
         cot_specs = [
@@ -187,12 +227,13 @@
     key_grads = [None] * levels
     value_grads = [None] * levels
     query_grad = None
+    probs = first_probs(infos[0], queries, key_rows)
     for level in reversed(range(levels)):
         first = min(level, levels - 2)
         if level == 0:
             gathered[0], *received = lax.optimization_barrier((gathered[0], *received))
         elif level < levels - 2:
-            gathered[level], dk = lax.optimization_barrier((gathered[level], dk))
+            gathered[level], dk, probs = lax.optimization_barrier((gathered[level], dk, probs))
         if level == 0:
             cot, weight = gathered[0], out_weight
         else:
@@ -203,7 +244,7 @@
             cot, weight = dout, None
         query_grad, dk, dv = attention_level(
             level, level - first, infos[level], queries, cot, weight,
-            key_rows, value_rows, kv_all, query_grad,
+            key_rows, value_rows, kv_all, query_grad, probs,
         )
         own = jnp.stack([dk[level], dv[level]])
         if level < levels - 1:

time: 358 us -> 358 us (level)
  waiting for transfers between devices: 155 us -> 148 us
  local copies, waits for them, and re-layouts: 24.5 us -> 28.8 us
    all_gather x3, waiting for transfers between devices: 68.6 us -> 61.3 us  [local(): gathered[first] = lax.all_gather(rows, 'head', axis=1, tiled=True)]
    unnamed x24 -> x28, local copies, waits for them, and re-layouts: 1.29 us -> 5.58 us
  transfers between devices with their start and end apart: 15 -> 15, of which waited for: 8 -> 8; matrix products, arithmetic and copies ran while one was open for 21% -> 21% of each run, Pallas kernels for 15% -> 16%
where the time goes in v5:
time: 358 us; the launch traced here: 357 us
  waiting for transfers between devices  148 us (41%)
  Pallas kernels  79.3 us (22%)
  matrix products  42.1 us (12%)
  between operations  30 us (8%)
  local copies, waits for them, and re-layouts  28.8 us (8%)
  other arithmetic  15.4 us (4%)
  starting transfers between devices  13.6 us (4%)
    ppermute x12, waiting for transfers between devices, swap(): return lax.ppermute(array, 'branch', pairs)  86.4 us
    pallas_call x4, Pallas kernels, attention_level(): pl.pallas_call(functools.partial(attention_kernel, level, fused, int(base...  76.5 us
    all_gather x3, waiting for transfers between devices, local(): gathered[first] = lax.all_gather(rows, 'head', axis=1, tiled=True)  61.3 us
    dot_general x2, matrix products, local(): lax.dot_general(gathered[first], out_weight, NT, preferred_element_type=j...  42.1 us
    ppermute x12, starting transfers between devices, swap(): return lax.ppermute(array, 'branch', pairs)  13.4 us
    concatenate x3, other arithmetic, local(): kv_all = jnp.concatenate([kv_all, swap(kv_all, bit)], axis=0)  8.15 us
  transfers between devices with their start and end apart: 15, of which 8 were waited for; matrix products, arithmetic and copies ran while one was open for 21% of the time, Pallas kernels for 16%

profile of v5, /device:TPU:0, one launch (start us, length us, event | category | flops | bytes accessed | tf_op | source)
XLA Modules:
  0.0 356.8 jit_solution(59210278913692463)
XLA Ops:
  7.2 3.2 slice.181
  10.4 3.1 fusion.17
  13.6 0.9 slice-done
  14.7 3.0 collective-permute-start
  17.8 17.5 %collective-permute-done = bf16[1,3,2,256,256]{4,3,2,1,0:T(8,128)(2,1)S(1)} collective-permute-done((bf16[1,3,2,256,256]{4,3,2,1,0:T(8,128)(2,1)S(1)}, bf16[1,3,2,256,256]{4,3,2,1,0:T(8,128)(2,1)S(1)}, u32[]{:S(2)}, u32[]{:S(2)}) %collective-permute-start) | collective-permute-done | bytes 786464 | tf_op jit(solution)/shard_map/ppermute | solution.py:196
  35.5 1.8 collective-permute-start.1
  37.3 34.0 %collective-permute-done.1 = bf16[2,3,2,256,256]{4,3,2,1,0:T(8,128)(2,1)S(1)} collective-permute-done((bf16[2,3,2,256,256]{4,3,2,1,0:T(8,128)(2,1)S(1)}, bf16[2,3,2,256,256]{4,3,2,1,0:T(8,128)(2,1)S(1)}, u32[]{:S(2)}, u32[]{:S(2)}) %collective-permute-start.1) | collective-permute-done | bytes 1572896 | tf_op jit(solution)/shard_map/ppermute | solution.py:196
  71.2 2.2 pad_maximum_fusion.1
  76.0 0.6 constant_dynamic-slice_fusion.13
  81.1 0.7 constant_dynamic-slice_fusion.12
  91.2 0.7 constant_dynamic-slice_fusion.10
  91.9 0.8 stack.44.info_ref
  92.7 2.2 copy-done
  94.9 2.8 first_probs.1.refs_1_
  97.6 2.1 copy-done.1
  99.7 1.3 stack.106.info_ref
  101.1 0.6 constant_dynamic-slice_fusion.9
  101.7 2.1 stack.103.info_ref
  103.8 2.6 stack.48.info_ref
  106.5 5.8 %pad_maximum_fusion.refs_0_.refs_1_.refs_2_.refs_4_.refs_5_.refs_6_.refs_3_ = bf16[8,3,2,256,256]{4,3,2,1,0:T(8,128)(2,1)} fusion(bf16[4,3,2,256,256]{4,3,2,1,0:T(8,128)(2,1)} %collective-permute-done.2, bf16[2,3,2,256,256]{4,3,2,1,0:T(8,128)(2,1)} %copy-done.5, bf16[1,3,2,256,256]{4,3,2,1,0:T(8,128)(2,1)S(1)} %collective-permute-done, ...), kind=kLoop, calls=%fused_computation | loop fusion | flops 9437184 | bytes 12582912 | tf_op jit(solution)/shard_map/concatenate | solution.py:207
  112.3 50.6 %all-gather.6.cloned.1.call-done = bf16[512,8192]{1,0:T(8,128)(2,1)} async-done(((bf16[512,2048]{1,0:T(8,128)(2,1)}), bf16[512,8192]{1,0:T(8,128)(2,1)}) %all-gather.6.cloned.1.call-update) | async-done | bytes 8388624 | tf_op jit(solution)/shard_map/all_gather | solution.py:203
  162.9 24.7 %convolution_convert_fusion.cot_ref = bf16[512,2048]{1,0:T(8,128)(2,1)} fusion(bf16[512,8192]{1,0:T(8,128)(2,1)} %all-gather.6.cloned.1.call-done, bf16[2048,8192]{1,0:T(8,128)(2,1)} %refs_0_.1), kind=kOutput, calls=%fused_computation.2 | convolution fusion | flops 17180917760 | bytes 44040192 | tf_op jit(solution)/shard_map/dot_general | solution.py:241
  187.6 22.5 %attention_level.4 = (bf16[4,1,256,2048]{3,2,1,0:T(8,128)(2,1)}, f32[4,256,256]{2,1,0:T(8,128)}, f32[4,256,256]{2,1,0:T(8,128)}) custom-call(s32[8]{0:T(128)S(1)} %stack.48.info_ref, bf16[4,1,256,2048]{3,2,1,0:T(8,128)(2,1)} %q_ref.9, bf16[512,2048]{1,0:T(8,128)(2,1)} %convolution_convert_fusion.cot_ref, ...), custom_call_target="tpu_custom_call" | custom-call | flops 21474836480 | bytes 3145728 | tf_op jit(solution)/shard_map/attention_level/pallas_call | solution.py:169
  210.2 2.1 fusion.18
  212.2 0.8 fusion.19
  213.1 1.2 select_convert_fusion
  214.4 18.3 %attention_level.5 = (bf16[4,1,256,2048]{3,2,1,0:T(8,128)(2,1)}, f32[3,256,256]{2,1,0:T(8,128)S(1)}, f32[3,256,256]{2,1,0:T(8,128)}) custom-call(s32[8]{0:T(128)S(1)} %stack.103.info_ref, bf16[4,1,256,2048]{3,2,1,0:T(8,128)(2,1)} %q_ref.9, bf16[512,2048]{1,0:T(8,128)(2,1)} %convolution_convert_fusion.cot_ref, ...), custom_call_target="tpu_custom_call", output_to_operand_aliasing={{0}: (9, {})} | custom-call | flops 16106127360 | bytes 3145728 | tf_op jit(solution)/shard_map/attention_level/pallas_call | solution.py:169
  232.7 10.7 %all-gather.10.cloned.1.call-done = bf16[1,1,256,8192]{3,2,1,0:T(8,128)(2,1)} async-done(((bf16[1,1,256,2048]{3,2,1,0:T(8,128)(2,1)}), bf16[1,1,256,8192]{3,2,1,0:T(8,128)(2,1)}) %all-gather.10.cloned.1.call-update) | async-done | bytes 4194320 | tf_op jit(solution)/shard_map/all_gather | solution.py:203
  243.4 17.3 %convolution_convert_fusion.1.cot_ref = bf16[256,2048]{1,0:T(8,128)(2,1)} fusion(bf16[256,8192]{1,0:T(8,128)(2,1)} %bitcast.49, bf16[2048,8192]{1,0:T(8,128)(2,1)} %refs_0_.1), kind=kOutput, calls=%fused_computation.3 | convolution fusion | flops 8590458880 | bytes 38797312 | tf_op jit(solution)/shard_map/dot_general | solution.py:241
  260.8 1.1 pad_maximum_fusion.3
  262.2 13.9 %attention_level.6 = (bf16[4,1,256,2048]{3,2,1,0:T(8,128)(2,1)}, f32[2,256,256]{2,1,0:T(8,128)S(1)}, f32[2,256,256]{2,1,0:T(8,128)S(1)}) custom-call(s32[8]{0:T(128)S(1)} %stack.106.info_ref, bf16[4,1,256,2048]{3,2,1,0:T(8,128)(2,1)} %q_ref.9, bf16[256,2048]{1,0:T(8,128)(2,1)} %convolution_convert_fusion.1.cot_ref, ...), custom_call_target="tpu_custom_call", output_to_operand_aliasing={{0}: (7, {})} | custom-call | flops 10737418240 | bytes 3145728 | tf_op jit(solution)/shard_map/attention_level/pallas_call | solution.py:169
  277.8 1.6 slice.255
  279.4 1.0 slice.256
  280.8 1.5 collective-permute-start.10
  282.4 0.6 fusion.16
  283.0 0.6 collective-permute-start.4
  284.1 1.5 collective-permute-start.7
  285.7 9.9 %collective-permute-done.10 = bf16[2,2,256,256]{3,2,1,0:T(8,128)(2,1)S(1)} collective-permute-done((bf16[2,2,256,256]{3,2,1,0:T(8,128)(2,1)S(1)}, bf16[2,2,256,256]{3,2,1,0:T(8,128)(2,1)S(1)}, u32[]{:S(2)}, u32[]{:S(2)}) %collective-permute-start.10) | collective-permute-done | bytes 524320 | tf_op jit(solution)/shard_map/ppermute | solution.py:196
  295.8 1.6 collective-permute-start.11
  297.3 9.5 %collective-permute-done.4 = bf16[2,2,256,256]{3,2,1,0:T(8,128)(2,1)S(1)} collective-permute-done((bf16[2,2,256,256]{3,2,1,0:T(8,128)(2,1)S(1)}, bf16[2,2,256,256]{3,2,1,0:T(8,128)(2,1)S(1)}, u32[]{:S(2)}, u32[]{:S(2)}) %collective-permute-start.4) | collective-permute-done | bytes 524320 | tf_op jit(solution)/shard_map/ppermute | solution.py:196
  307.0 1.6 collective-permute-start.5
  308.6 9.1 %collective-permute-done.7 = bf16[2,2,256,256]{3,2,1,0:T(8,128)(2,1)S(1)} collective-permute-done((bf16[2,2,256,256]{3,2,1,0:T(8,128)(2,1)S(1)}, bf16[2,2,256,256]{3,2,1,0:T(8,128)(2,1)S(1)}, u32[]{:S(2)}, u32[]{:S(2)}) %collective-permute-start.7) | collective-permute-done | bytes 524320 | tf_op jit(solution)/shard_map/ppermute | solution.py:196
  317.8 1.6 collective-permute-start.8
  319.5 6.3 %collective-permute-done.8 = bf16[1,2,256,256]{3,2,1,0:T(8,128)(2,1)S(1)} collective-permute-done((bf16[1,2,256,256]{3,2,1,0:T(8,128)(2,1)S(1)}, bf16[1,2,256,256]{3,2,1,0:T(8,128)(2,1)S(1)}, u32[]{:S(2)}, u32[]{:S(2)}) %collective-permute-start.8) | collective-permute-done | bytes 262176 | tf_op jit(solution)/shard_map/ppermute | solution.py:196
  326.0 21.7 %attention_level.7 = (bf16[4,1,256,2048]{3,2,1,0:T(8,128)(2,1)}, f32[1,256,256]{2,1,0:T(8,128)S(1)}, f32[1,256,256]{2,1,0:T(8,128)S(1)}) custom-call(s32[8]{0:T(128)S(1)} %stack.44.info_ref, bf16[4,1,256,2048]{3,2,1,0:T(8,128)(2,1)} %q_ref.9, bf16[256,8192]{1,0:T(8,128)(2,1)} %bitcast.48, ...), custom_call_target="tpu_custom_call", output_to_operand_aliasing={{0}: (7, {})} | custom-call | flops 13958643712 | bytes 3145728 | tf_op jit(solution)/shard_map/attention_level/pallas_call | solution.py:169
  347.8 0.7 copy-done.10
  348.6 0.9 maximum_bitcast_fusion.2
  349.5 0.9 maximum_bitcast_fusion.1
  (85 shorter events, 4.9 us)
Async XLA Ops:
  7.2 155.7 %all-gather.6.cloned.1.call-start = ((), (), s32[]{:S(2)}) async-start(), calls=%async_computation | async-start | bytes 10485760 | tf_op jit(solution)/shard_map/all_gather | solution.py:203
  10.4 233.0 %all-gather.10.cloned.1.call-start = ((), (), s32[]{:S(2)}) async-start(), calls=%async_computation.2 | async-start | bytes 5242880 | tf_op jit(solution)/shard_map/all_gather | solution.py:203
  13.5 1.0 slice-start
  13.5 1.1 slice-start.1
  13.6 312.4 %all-gather.8.cloned.1.call-start = ((), (), s32[]{:S(2)}) async-start(), calls=%async_computation.1 | async-start | bytes 5242880 | tf_op jit(solution)/shard_map/all_gather | solution.py:203
  14.7 20.6 %collective-permute-start = (bf16[1,3,2,256,256]{4,3,2,1,0:T(8,128)(2,1)S(1)}, bf16[1,3,2,256,256]{4,3,2,1,0:T(8,128)(2,1)S(1)}, u32[]{:S(2)}, u32[]{:S(2)}) collective-permute-start(bf16[1,3,2,256,256]{4,3,2,1,0:T(8,128)(2,1)S(1)} %maximum_bitcast_fusion), channel_id=1, source_target_pairs={{0,16},{4,20},{8,24},{12,28},{16,0},{20,4},{24,8},{28,12},{1,17},{... | collective-permute-start | bytes 2359304 | tf_op jit(solution)/shard_map/ppermute | solution.py:196
  35.4 38.0 %copy-start.12 = (s32[3,8]{1,0:T(4,128)S(1)}, s32[3,8]{1,0:T(4,128)}, u32[]{:S(2)}) copy-start(s32[3,8]{1,0:T(4,128)} %param.24) | copy-start | bytes 292
  35.5 55.7 %copy-start.11 = (s32[4,8]{1,0:T(4,128)S(1)}, s32[4,8]{1,0:T(4,128)}, u32[]{:S(2)}) copy-start(s32[4,8]{1,0:T(4,128)} %param.25) | copy-start | bytes 388
  35.5 57.2 %copy-start.2 = (bf16[4,1,256,256]{3,2,1,0:T(8,128)(2,1)S(1)}, bf16[4,1,256,256]{3,2,1,0:T(8,128)(2,1)}, u32[]{:S(2)}) copy-start(bf16[4,1,256,256]{3,2,1,0:T(8,128)(2,1)} %refs_2_.3) | copy-start | bytes 1572868
  35.5 35.8 %collective-permute-start.1 = (bf16[2,3,2,256,256]{4,3,2,1,0:T(8,128)(2,1)S(1)}, bf16[2,3,2,256,256]{4,3,2,1,0:T(8,128)(2,1)S(1)}, u32[]{:S(2)}, u32[]{:S(2)}) collective-permute-start(bf16[2,3,2,256,256]{4,3,2,1,0:T(8,128)(2,1)S(1)} %pad_maximum_fusion.2), channel_id=1, source_target_pairs={{0,8},{4,12},{8,0},{12,4},{16,24},{20,28},{24,16},{28,20},{1,9},{5... | collective-permute-start | bytes 4718600 | tf_op jit(solution)/shard_map/ppermute | solution.py:196
  71.2 2.2 copy-start.5
  73.4 33.0 %collective-permute-start.2 = (bf16[4,3,2,256,256]{4,3,2,1,0:T(8,128)(2,1)}, bf16[4,3,2,256,256]{4,3,2,1,0:T(8,128)(2,1)}, u32[]{:S(2)}, u32[]{:S(2)}) collective-permute-start(bf16[4,3,2,256,256]{4,3,2,1,0:T(8,128)(2,1)} %pad_maximum_fusion.1), channel_id=1, source_target_pairs={{0,4},{4,0},{8,12},{12,8},{16,20},{20,16},{24,28},{28,24},{1,5},{5... | collective-permute-start | bytes 9437192 | tf_op jit(solution)/shard_map/ppermute | solution.py:196
  92.7 2.2 copy-start
  94.8 11.6 %copy-start.13 = (s32[4]{0:T(128)S(1)}, s32[4]{0:T(128)}, u32[]{:S(2)}) copy-start(s32[4]{0:T(128)} %constant.86.clone) | copy-start | bytes 52
  97.6 2.1 copy-start.1
  112.3 75.3 %copy-start.3 = (bf16[4,1,256,256]{3,2,1,0:T(8,128)(2,1)S(1)}, bf16[4,1,256,256]{3,2,1,0:T(8,128)(2,1)}, u32[]{:S(2)}) copy-start(bf16[4,1,256,256]{3,2,1,0:T(8,128)(2,1)} %refs_3_.5) | copy-start | bytes 1572868
  210.2 2.1 copy-start.8
  214.3 66.1 %collective-permute-start.9 = (bf16[4,2,256,256]{3,2,1,0:T(8,128)(2,1)}, bf16[4,2,256,256]{3,2,1,0:T(8,128)(2,1)S(1)}, u32[]{:S(2)}, u32[]{:S(2)}) collective-permute-start(bf16[4,2,256,256]{3,2,1,0:T(8,128)(2,1)} %select_convert_fusion), channel_id=1, source_target_pairs={{0,4},{4,0},{8,12},{12,8},{16,20},{20,16},{24,28},{28,24},{1,5},{5... | collective-permute-start | bytes 3145736 | tf_op jit(solution)/shard_map/ppermute | solution.py:196
  260.8 1.3 copy-start.9
  276.1 1.0 copy-start.6
  276.1 1.0 copy-start.7
  276.7 5.7 %collective-permute-start.3 = (bf16[4,2,256,256]{3,2,1,0:T(8,128)(2,1)S(1)}, bf16[4,2,256,256]{3,2,1,0:T(8,128)(2,1)S(1)}, u32[]{:S(2)}, u32[]{:S(2)}) collective-permute-start(bf16[4,2,256,256]{3,2,1,0:T(8,128)(2,1)S(1)} %add_convert_fusion.1), channel_id=1, source_target_pairs={{0,4},{4,0},{8,12},{12,8},{16,20},{20,16},{24,28},{28,24},{1,5},{5... | collective-permute-start | bytes 3145736 | tf_op jit(solution)/shard_map/ppermute | solution.py:196
  277.6 6.0 %collective-permute-start.6 = (bf16[4,2,256,256]{3,2,1,0:T(8,128)(2,1)S(1)}, bf16[4,2,256,256]{3,2,1,0:T(8,128)(2,1)S(1)}, u32[]{:S(2)}, u32[]{:S(2)}) collective-permute-start(bf16[4,2,256,256]{3,2,1,0:T(8,128)(2,1)S(1)} %add_convert_fusion), channel_id=1, source_target_pairs={{0,4},{4,0},{8,12},{12,8},{16,20},{20,16},{24,28},{28,24},{1,5},{5... | collective-permute-start | bytes 3145736 | tf_op jit(solution)/shard_map/ppermute | solution.py:196
  280.8 14.8 %collective-permute-start.10 = (bf16[2,2,256,256]{3,2,1,0:T(8,128)(2,1)S(1)}, bf16[2,2,256,256]{3,2,1,0:T(8,128)(2,1)S(1)}, u32[]{:S(2)}, u32[]{:S(2)}) collective-permute-start(bf16[2,2,256,256]{3,2,1,0:T(8,128)(2,1)S(1)} %slice.206), channel_id=1, source_target_pairs={{0,8},{4,12},{8,0},{12,4},{16,24},{20,28},{24,16},{28,20},{1,9},{5... | collective-permute-start | bytes 1572872 | tf_op jit(solution)/shard_map/ppermute | solution.py:196
  283.0 23.8 %collective-permute-start.4 = (bf16[2,2,256,256]{3,2,1,0:T(8,128)(2,1)S(1)}, bf16[2,2,256,256]{3,2,1,0:T(8,128)(2,1)S(1)}, u32[]{:S(2)}, u32[]{:S(2)}) collective-permute-start(bf16[2,2,256,256]{3,2,1,0:T(8,128)(2,1)S(1)} %slice.192), channel_id=1, source_target_pairs={{0,8},{4,12},{8,0},{12,4},{16,24},{20,28},{24,16},{28,20},{1,9},{5... | collective-permute-start | bytes 1572872 | tf_op jit(solution)/shard_map/ppermute | solution.py:196
  284.1 33.5 %collective-permute-start.7 = (bf16[2,2,256,256]{3,2,1,0:T(8,128)(2,1)S(1)}, bf16[2,2,256,256]{3,2,1,0:T(8,128)(2,1)S(1)}, u32[]{:S(2)}, u32[]{:S(2)}) collective-permute-start(bf16[2,2,256,256]{3,2,1,0:T(8,128)(2,1)S(1)} %slice.200), channel_id=1, source_target_pairs={{0,8},{4,12},{8,0},{12,4},{16,24},{20,28},{24,16},{28,20},{1,9},{5... | collective-permute-start | bytes 1572872 | tf_op jit(solution)/shard_map/ppermute | solution.py:196
  295.8 23.6 %collective-permute-start.11 = (bf16[1,2,256,256]{3,2,1,0:T(8,128)(2,1)S(1)}, bf16[1,2,256,256]{3,2,1,0:T(8,128)(2,1)S(1)}, u32[]{:S(2)}, u32[]{:S(2)}) collective-permute-start(bf16[1,2,256,256]{3,2,1,0:T(8,128)(2,1)S(1)} %slice.252), channel_id=1, source_target_pairs={{0,16},{4,20},{8,24},{12,28},{16,0},{20,4},{24,8},{28,12},{1,17},{... | collective-permute-start | bytes 786440 | tf_op jit(solution)/shard_map/ppermute | solution.py:196
  307.0 12.3 %collective-permute-start.5 = (bf16[1,2,256,256]{3,2,1,0:T(8,128)(2,1)S(1)}, bf16[1,2,256,256]{3,2,1,0:T(8,128)(2,1)S(1)}, u32[]{:S(2)}, u32[]{:S(2)}) collective-permute-start(bf16[1,2,256,256]{3,2,1,0:T(8,128)(2,1)S(1)} %slice.254), channel_id=1, source_target_pairs={{0,16},{4,20},{8,24},{12,28},{16,0},{20,4},{24,8},{28,12},{1,17},{... | collective-permute-start | bytes 786440 | tf_op jit(solution)/shard_map/ppermute | solution.py:196
  317.8 8.2 %copy-start.4 = (bf16[4,1,256,256]{3,2,1,0:T(8,128)(2,1)S(1)}, bf16[4,1,256,256]{3,2,1,0:T(8,128)(2,1)}, u32[]{:S(2)}) copy-start(bf16[4,1,256,256]{3,2,1,0:T(8,128)(2,1)} %refs_3_.5) | copy-start | bytes 1572868
  317.8 8.0 %collective-permute-start.8 = (bf16[1,2,256,256]{3,2,1,0:T(8,128)(2,1)S(1)}, bf16[1,2,256,256]{3,2,1,0:T(8,128)(2,1)S(1)}, u32[]{:S(2)}, u32[]{:S(2)}) collective-permute-start(bf16[1,2,256,256]{3,2,1,0:T(8,128)(2,1)S(1)} %slice.253), channel_id=1, source_target_pairs={{0,16},{4,20},{8,24},{12,28},{16,0},{20,4},{24,8},{28,12},{1,17},{... | collective-permute-start | bytes 786440 | tf_op jit(solution)/shard_map/ppermute | solution.py:196
  347.7 0.9 copy-start.10
Sparse Core Ops, SparseCore 0:
  10.5 152.3 all-gather.5
  164.5 78.9 all-gather.9
  245.0 79.2 all-gather.7
